TPU v7x, 512 devices: a whole 4x8x8 slice. The times are simulated.
512 devices in a mesh: cp: 128 (over z_hi, y, x), hd: 4 (over z_lo, core).
Axes of the slice: x: 4, y: 8, z: 8 (z_hi: 4, z_lo: 2; z = z_hi * 2 + z_lo), core: 2. Of those that a mesh axis runs over, the one named last changes fastest.
Arguments:
- queries: bfloat16 [98304, 8, 128], P('cp', 'hd'), may hold values from -384 to 384
- keys_values: bfloat16 [2, 98304, 128], P(None, ('cp', 'hd')), may hold values from -32 to 32
- doc_start: int32 [98304], P('cp'), may hold values from 0 to 98303, as said below
Outputs:
- attended: bfloat16 [98304, 8, 128], P('cp', 'hd')
- log_total: float32 [8, 98304], P('hd', 'cp')
Inputs may be any that keep to these rules, and one draw needn't show every extreme that they name: doc_start[t] is the first position of the document holding token t; documents are contiguous runs and never cross a boundary between aligned groups of 4 shards of 768 tokens, so a token's document starts at most 3 shards before the token's own shard, and in every draw some document reaches exactly that far.
All inputs are finite; a program needn't handle non-finite values.
Results may differ from a plain program's by a relative error of at most 0.015.
Values may be sent and summed in bfloat16 or wider, within the bound.
No kernel may reach another device: no remote copies, remote signals or barrier semaphores. Data moves between devices by JAX's collectives and lax.ppermute only.
A program may use at most 64 MiB of HBM per device.

v0:
```python
import math

import jax
import jax.numpy as jnp
from jax import lax
from jax.sharding import PartitionSpec as P

REACH = 3


MASKED_SCORE = -1e30


def passed_along(value, axis, steps):
    count = lax.axis_size(axis)
    first, last = (max(0, -steps), min(count, count - steps))
    return lax.ppermute(value, axis, [(source, source + steps) for source in range(first, last)])


def from_behind(value, axis, steps):
    count = lax.axis_size(axis)
    pairs = [(source, (source + steps) % count) for source in range(count)]
    return lax.ppermute(value, axis, pairs)


def attend_piece(carried, queries, starts, q_first, key_rows, values, k_first):
    row_peak, row_total, weighted = carried
    query_count = queries.shape[0]
    key_count = key_rows.shape[0]
    score_scale = queries.shape[2] ** (-0.5)
    scores = (
        jnp.einsum("qhd,kd->hqk", queries, key_rows, preferred_element_type=jnp.float32)
        * score_scale
    )
    q_pos = q_first + jnp.arange(query_count, dtype=jnp.int32)
    k_pos = k_first + jnp.arange(key_count, dtype=jnp.int32)
    visible = (k_pos[None, :] <= q_pos[:, None]) & (k_pos[None, :] >= starts[:, None])
    scores = jnp.where(visible[None], scores, MASKED_SCORE)
    fresh_peak = jnp.maximum(row_peak, jnp.max(scores, axis=-1))
    weights = jnp.where(visible[None], jnp.exp(scores - fresh_peak[..., None]), 0.0)
    factor = jnp.exp(row_peak - fresh_peak)
    row_total = row_total * factor + jnp.sum(weights, axis=-1)
    weighted = weighted * factor[..., None] + jnp.einsum(
        "hqk,kd->hqd", weights.astype(jnp.bfloat16), values, preferred_element_type=jnp.float32
    )
    return (fresh_peak, row_total, weighted)


def attend_block(carried, queries, starts, q_first, paired, k_first):
    total_len = paired.shape[1]
    step_len = math.gcd(total_len, 256)
    for offset in range(0, total_len, step_len):
        carried = attend_piece(
            carried,
            queries,
            starts,
            q_first,
            paired[0, offset : offset + step_len],
            paired[1, offset : offset + step_len],
            k_first + offset,
        )
    return carried


def attend_maybe(carried, queries, starts, q_first, paired, k_first):
    return attend_block(carried, queries, starts, q_first, paired, k_first)


def per_device(queries, keys_values, doc_start):
    pieces = lax.all_gather(keys_values, "hd", axis=1, tiled=True)
    query_count = queries.shape[0]
    head_count = queries.shape[1]
    head_width = queries.shape[2]
    shard_count = lax.axis_size("cp")
    shard_index = lax.axis_index("cp")
    own_first = shard_index * query_count
    start_state = (
        jnp.full((head_count, query_count), MASKED_SCORE, jnp.float32),
        jnp.zeros((head_count, query_count), jnp.float32),
        jnp.zeros((head_count, query_count, head_width), jnp.float32),
    )
    carried = attend_block(start_state, queries, doc_start, own_first, pieces, own_first)
    travel_q = queries
    travel_starts = doc_start.astype(jnp.float32)
    for distance in range(1, REACH + 1):
        travel_q = passed_along(travel_q, "cp", -1)
        moved = from_behind((carried[0], carried[1], carried[2], travel_starts), "cp", -1)
        carried = (moved[0], moved[1], moved[2])
        travel_starts = moved[3]
        anchor = (shard_index + distance) % shard_count
        starts = travel_starts.astype(jnp.int32)
        carried = attend_maybe(carried, travel_q, starts, anchor * query_count, pieces, own_first)
    carried = (
        from_behind(carried[0].astype(jnp.bfloat16), "cp", REACH).astype(jnp.float32),
        from_behind(carried[1].astype(jnp.bfloat16), "cp", REACH).astype(jnp.float32),
        from_behind(carried[2].astype(jnp.bfloat16), "cp", REACH).astype(jnp.float32),
    )
    row_peak, row_total, weighted = carried
    attended = (weighted / row_total[..., None]).transpose(1, 0, 2).astype(jnp.bfloat16)
    log_total = row_peak + jnp.log(row_total)
    return (attended, log_total)


def solution(mesh):
    return jax.shard_map(
        per_device,
        mesh=mesh,
        in_specs=(P("cp", "hd", None), P(None, ("cp", "hd"), None), P("cp")),
        out_specs=(P("cp", "hd", None), P("hd", "cp")),
        check_vma=False,
    )
```

profile of v0, /device:TPU:178, one launch (start us, length us, event | category | flops | bytes accessed | tf_op | source)
XLA Modules:
  0.0 225.8 jit_solution(7478718750851408695)
XLA Ops:
  1.3 2.4 %collective-permute-start.2 = (f32[768]{0:T(1024)S(1)}, f32[768]{0:T(1024)S(1)}, u32[]{:S(2)}, u32[]{:S(2)}) collective-permute-start(f32[768]{0:T(1024)S(1)} %convert_element_type.75), channel_id=1, source_target_pairs={{0,508},{4,0},{8,4},{12,8},{16,12},{20,16},{24,20},{28,24},{32,28}... | collective-permute-start | bytes 9224 | tf_op jit(solution)/shard_map/ppermute | solution.py:23
  4.8 5.6 %collective-permute-start.3 = (bf16[768,2,128]{2,0,1:T(8,128)(2,1)S(1)}, bf16[768,2,128]{2,0,1:T(8,128)(2,1)S(1)}, u32[]{:S(2)}, u32[]{:S(2)}) collective-permute-start(bf16[768,2,128]{2,0,1:T(8,128)(2,1)S(1)} %copy.5), channel_id=1, source_target_pairs={{4,0},{8,4},{12,8},{16,12},{20,16},{24,20},{28,24},{32,28},{36,32}... | collective-permute-start | bytes 1179656 | tf_op jit(solution)/shard_map/ppermute | solution.py:17
  10.5 7.6 %all_gather.3 = bf16[2,768,128]{2,1,0:T(8,128)(2,1)S(1)} all-gather(bf16[2,192,128]{2,1,0:T(8,128)(2,1)} %param.4), channel_id=1, replica_groups=mesh['cp'=128,'hd'=4] {'hd'}, dimensions={1}, use_global_device_ids=true | all-gather | bytes 491520 | tf_op jit(solution)/shard_map/all_gather | solution.py:70
  18.1 2.7 %collective-permute-start.6 = (f32[768]{0:T(1024)S(1)}, f32[768]{0:T(1024)S(1)}, u32[]{:S(2)}, u32[]{:S(2)}) collective-permute-start(f32[768]{0:T(1024)S(1)} %collective-permute-done.2), channel_id=1, source_target_pairs={{0,508},{4,0},{8,4},{12,8},{16,12},{20,16},{24,20},{28,24},{32,28}... | collective-permute-start | bytes 9224 | tf_op jit(solution)/shard_map/ppermute | solution.py:23
  20.8 2.7 %collective-permute-done.6 = f32[768]{0:T(1024)S(1)} collective-permute-done((f32[768]{0:T(1024)S(1)}, f32[768]{0:T(1024)S(1)}, u32[]{:S(2)}, u32[]{:S(2)}) %collective-permute-start.6) | collective-permute-done | bytes 3104 | tf_op jit(solution)/shard_map/ppermute | solution.py:23
  23.6 2.7 %collective-permute-start.10 = (f32[768]{0:T(1024)S(1)}, f32[768]{0:T(1024)S(1)}, u32[]{:S(2)}, u32[]{:S(2)}) collective-permute-start(f32[768]{0:T(1024)S(1)} %collective-permute-done.6), channel_id=1, source_target_pairs={{0,508},{4,0},{8,4},{12,8},{16,12},{20,16},{24,20},{28,24},{32,28}... | collective-permute-start | bytes 9224 | tf_op jit(solution)/shard_map/ppermute | solution.py:23
  26.3 2.7 %collective-permute-done.10 = f32[768]{0:T(1024)S(1)} collective-permute-done((f32[768]{0:T(1024)S(1)}, f32[768]{0:T(1024)S(1)}, u32[]{:S(2)}, u32[]{:S(2)}) %collective-permute-start.10) | collective-permute-done | bytes 3104 | tf_op jit(solution)/shard_map/ppermute | solution.py:23
  29.0 3.0 %compare_and_fusion.11 = (pred[768,256]{0,1:T(8,128)(4,1)S(1)}, pred[768,256]{0,1:T(8,128)(4,1)S(1)}, pred[768,256]{0,1:T(8,128)(4,1)S(1)}, pred[768,256]{0,1:T(...) fusion(s32[768]{0:T(1024)} %param.5, ...), kind=kLoop, calls=%fused_computation.113 | loop fusion | flops 7077888 | bytes 2386944 | tf_op jit(solution)/shard_map/and | solution.py:37
  33.5 3.1 %collective-permute-start.1 = (f32[2,768]{1,0:T(2,128)S(1)}, f32[2,768]{1,0:T(2,128)S(1)}, u32[]{:S(2)}, u32[]{:S(2)}) collective-permute-start(f32[2,768]{1,0:T(2,128)S(1)} %get-tuple-element.29), channel_id=1, source_target_pairs={{0,508},{4,0},{8,4},{12,8},{16,12},{20,16},{24,20},{28,24},{32,28}... | collective-permute-start | bytes 18440 | tf_op jit(solution)/shard_map/ppermute | solution.py:23
  37.6 6.3 %collective-permute-start.13 = (f32[2,768]{1,0:T(2,128)S(1)}, f32[2,768]{1,0:T(2,128)S(1)}, u32[]{:S(2)}, u32[]{:S(2)}) collective-permute-start(f32[2,768]{1,0:T(2,128)S(1)} %get-tuple-element.20), channel_id=1, source_target_pairs={{0,508},{4,0},{8,4},{12,8},{16,12},{20,16},{24,20},{28,24},{32,28}... | collective-permute-start | bytes 18440 | tf_op jit(solution)/shard_map/ppermute | solution.py:23
  45.9 1.9 collective-permute-start
  49.2 2.5 %collective-permute-done.1 = f32[2,768]{1,0:T(2,128)S(1)} collective-permute-done((f32[2,768]{1,0:T(2,128)S(1)}, f32[2,768]{1,0:T(2,128)S(1)}, u32[]{:S(2)}, u32[]{:S(2)}) %collective-permute-start.1) | collective-permute-done | bytes 6176 | tf_op jit(solution)/shard_map/ppermute | solution.py:23
  51.7 1.9 collective-permute-start.5
  55.3 1.9 collective-permute-start.7
  57.2 4.9 %collective-permute-start.14 = (f32[2,768]{1,0:T(2,128)S(1)}, f32[2,768]{1,0:T(2,128)S(1)}, u32[]{:S(2)}, u32[]{:S(2)}) collective-permute-start(f32[2,768]{1,0:T(2,128)S(1)} %get-tuple-element.16), channel_id=1, source_target_pairs={{0,508},{4,0},{8,4},{12,8},{16,12},{20,16},{24,20},{28,24},{32,28}... | collective-permute-start | bytes 18440 | tf_op jit(solution)/shard_map/ppermute | solution.py:23
  62.7 19.2 %collective-permute-done.7 = bf16[768,2,128]{2,0,1:T(8,128)(2,1)S(1)} collective-permute-done((bf16[768,2,128]{2,0,1:T(8,128)(2,1)S(1)}, bf16[768,2,128]{2,0,1:T(8,128)(2,1)S(1)}, u32[]{:S(2)}, u32[]{:S(2)}) %collective-permute-start.7) | collective-permute-done | bytes 393248 | tf_op jit(solution)/shard_map/ppermute | solution.py:17
  83.4 2.1 collective-permute-start.9
  94.5 9.0 %collective-permute-done.11 = bf16[768,2,128]{2,0,1:T(8,128)(2,1)S(1)} collective-permute-done((bf16[768,2,128]{2,0,1:T(8,128)(2,1)S(1)}, bf16[768,2,128]{2,0,1:T(8,128)(2,1)S(1)}, u32[]{:S(2)}, u32[]{:S(2)}) %collective-permute-start.11) | collective-permute-done | bytes 393248 | tf_op jit(solution)/shard_map/ppermute | solution.py:17
  105.9 11.5 %collective-permute-done.4 = f32[2,768,128]{2,1,0:T(8,128)S(1)} collective-permute-done((f32[2,768,128]{2,1,0:T(8,128)S(1)}, f32[2,768,128]{2,1,0:T(8,128)S(1)}, u32[]{:S(2)}, u32[]{:S(2)}) %collective-permute-start.4) | collective-permute-done | bytes 786464 | tf_op jit(solution)/shard_map/ppermute | solution.py:23
  118.3 1.9 collective-permute-start.8
  121.6 16.6 %collective-permute-done.8 = f32[2,768,128]{2,1,0:T(8,128)S(1)} collective-permute-done((f32[2,768,128]{2,1,0:T(8,128)S(1)}, f32[2,768,128]{2,1,0:T(8,128)S(1)}, u32[]{:S(2)}, u32[]{:S(2)}) %collective-permute-start.8) | collective-permute-done | bytes 786464 | tf_op jit(solution)/shard_map/ppermute | solution.py:23
  139.3 6.3 %collective-permute-start.12 = (bf16[2,768,128]{2,1,0:T(8,128)(2,1)S(1)}, bf16[2,768,128]{2,1,0:T(8,128)(2,1)S(1)}, u32[]{:S(2)}, u32[]{:S(2)}) collective-permute-start(bf16[2,768,128]{2,1,0:T(8,128)(2,1)S(1)} %add_convert_fusion), channel_id=1, source_target_pairs={{0,12},{4,16},{8,20},{12,24},{16,28},{20,32},{24,36},{28,40},{32,4... | collective-permute-start | bytes 1179656 | tf_op jit(solution)/shard_map/ppermute | solution.py:23
  145.6 71.7 %collective-permute-start.16 = (bf16[2,768]{1,0:T(2,128)(2,1)S(1)}, bf16[2,768]{1,0:T(2,128)(2,1)S(1)}, u32[]{:S(2)}, u32[]{:S(2)}) collective-permute-start(bf16[2,768]{1,0:T(2,128)(2,1)S(1)} %get-tuple-element.8), channel_id=1, source_target_pairs={{0,12},{4,16},{8,20},{12,24},{16,28},{20,32},{24,36},{28,40},{32,4... | collective-permute-start | bytes 9224 | tf_op jit(solution)/shard_map/ppermute | solution.py:23
  219.3 4.4 %collective-permute-done.17 = bf16[2,768]{1,0:T(2,128)(2,1)S(1)} collective-permute-done((bf16[2,768]{1,0:T(2,128)(2,1)S(1)}, bf16[2,768]{1,0:T(2,128)(2,1)S(1)}, u32[]{:S(2)}, u32[]{:S(2)}) %collective-permute-start.17) | collective-permute-done | bytes 3104 | tf_op jit(solution)/shard_map/ppermute | solution.py:23
  (72 shorter events, 29.9 us)
Async XLA Ops:
  1.3 16.7 %collective-permute-start.2 = (f32[768]{0:T(1024)S(1)}, f32[768]{0:T(1024)S(1)}, u32[]{:S(2)}, u32[]{:S(2)}) collective-permute-start(f32[768]{0:T(1024)S(1)} %convert_element_type.75), channel_id=1, source_target_pairs={{0,508},{4,0},{8,4},{12,8},{16,12},{20,16},{24,20},{28,24},{32,28}... | collective-permute-start | bytes 9224 | tf_op jit(solution)/shard_map/ppermute | solution.py:23
  4.8 27.2 %copy-start = (bf16[768,2,128]{2,1,0:T(2,128)(2,1)S(1)}, bf16[768,2,128]{2,1,0:T(2,128)(2,1)}, u32[]{:S(2)}) copy-start(bf16[768,2,128]{2,1,0:T(2,128)(2,1)} %param.3) | copy-start | bytes 1179652
  4.8 43.0 %collective-permute-start.3 = (bf16[768,2,128]{2,0,1:T(8,128)(2,1)S(1)}, bf16[768,2,128]{2,0,1:T(8,128)(2,1)S(1)}, u32[]{:S(2)}, u32[]{:S(2)}) collective-permute-start(bf16[768,2,128]{2,0,1:T(8,128)(2,1)S(1)} %copy.5), channel_id=1, source_target_pairs={{4,0},{8,4},{12,8},{16,12},{20,16},{24,20},{28,24},{32,28},{36,32}... | collective-permute-start | bytes 1179656 | tf_op jit(solution)/shard_map/ppermute | solution.py:17
  18.1 5.5 %collective-permute-start.6 = (f32[768]{0:T(1024)S(1)}, f32[768]{0:T(1024)S(1)}, u32[]{:S(2)}, u32[]{:S(2)}) collective-permute-start(f32[768]{0:T(1024)S(1)} %collective-permute-done.2), channel_id=1, source_target_pairs={{0,508},{4,0},{8,4},{12,8},{16,12},{20,16},{24,20},{28,24},{32,28}... | collective-permute-start | bytes 9224 | tf_op jit(solution)/shard_map/ppermute | solution.py:23
  23.6 5.5 %collective-permute-start.10 = (f32[768]{0:T(1024)S(1)}, f32[768]{0:T(1024)S(1)}, u32[]{:S(2)}, u32[]{:S(2)}) collective-permute-start(f32[768]{0:T(1024)S(1)} %collective-permute-done.6), channel_id=1, source_target_pairs={{0,508},{4,0},{8,4},{12,8},{16,12},{20,16},{24,20},{28,24},{32,28}... | collective-permute-start | bytes 9224 | tf_op jit(solution)/shard_map/ppermute | solution.py:23
  33.5 18.2 %collective-permute-start.1 = (f32[2,768]{1,0:T(2,128)S(1)}, f32[2,768]{1,0:T(2,128)S(1)}, u32[]{:S(2)}, u32[]{:S(2)}) collective-permute-start(f32[2,768]{1,0:T(2,128)S(1)} %get-tuple-element.29), channel_id=1, source_target_pairs={{0,508},{4,0},{8,4},{12,8},{16,12},{20,16},{24,20},{28,24},{32,28}... | collective-permute-start | bytes 18440 | tf_op jit(solution)/shard_map/ppermute | solution.py:23
  37.6 19.6 %collective-permute-start.13 = (f32[2,768]{1,0:T(2,128)S(1)}, f32[2,768]{1,0:T(2,128)S(1)}, u32[]{:S(2)}, u32[]{:S(2)}) collective-permute-start(f32[2,768]{1,0:T(2,128)S(1)} %get-tuple-element.20), channel_id=1, source_target_pairs={{0,508},{4,0},{8,4},{12,8},{16,12},{20,16},{24,20},{28,24},{32,28}... | collective-permute-start | bytes 18440 | tf_op jit(solution)/shard_map/ppermute | solution.py:23
  45.9 45.7 %collective-permute-start = (f32[2,768,128]{2,1,0:T(8,128)S(1)}, f32[2,768,128]{2,1,0:T(8,128)S(1)}, u32[]{:S(2)}, u32[]{:S(2)}) collective-permute-start(f32[2,768,128]{2,1,0:T(8,128)S(1)} %convolution_add_fusion), channel_id=1, source_target_pairs={{0,508},{4,0},{8,4},{12,8},{16,12},{20,16},{24,20},{28,24},{32,28}... | collective-permute-start | bytes 2359304 | tf_op jit(solution)/shard_map/ppermute | solution.py:23
  51.7 31.6 %collective-permute-start.5 = (f32[2,768]{1,0:T(2,128)S(1)}, f32[2,768]{1,0:T(2,128)S(1)}, u32[]{:S(2)}, u32[]{:S(2)}) collective-permute-start(f32[2,768]{1,0:T(2,128)S(1)} %get-tuple-element.26), channel_id=1, source_target_pairs={{0,508},{4,0},{8,4},{12,8},{16,12},{20,16},{24,20},{28,24},{32,28}... | collective-permute-start | bytes 18440 | tf_op jit(solution)/shard_map/ppermute | solution.py:23
  55.3 26.7 %collective-permute-start.7 = (bf16[768,2,128]{2,0,1:T(8,128)(2,1)S(1)}, bf16[768,2,128]{2,0,1:T(8,128)(2,1)S(1)}, u32[]{:S(2)}, u32[]{:S(2)}) collective-permute-start(bf16[768,2,128]{2,0,1:T(8,128)(2,1)S(1)} %collective-permute-done.3), channel_id=1, source_target_pairs={{4,0},{8,4},{12,8},{16,12},{20,16},{24,20},{28,24},{32,28},{36,32}... | collective-permute-start | bytes 1179656 | tf_op jit(solution)/shard_map/ppermute | solution.py:17
  57.2 32.4 %collective-permute-start.14 = (f32[2,768]{1,0:T(2,128)S(1)}, f32[2,768]{1,0:T(2,128)S(1)}, u32[]{:S(2)}, u32[]{:S(2)}) collective-permute-start(f32[2,768]{1,0:T(2,128)S(1)} %get-tuple-element.16), channel_id=1, source_target_pairs={{0,508},{4,0},{8,4},{12,8},{16,12},{20,16},{24,20},{28,24},{32,28}... | collective-permute-start | bytes 18440 | tf_op jit(solution)/shard_map/ppermute | solution.py:23
  83.4 21.5 %collective-permute-start.9 = (f32[2,768]{1,0:T(2,128)S(1)}, f32[2,768]{1,0:T(2,128)S(1)}, u32[]{:S(2)}, u32[]{:S(2)}) collective-permute-start(f32[2,768]{1,0:T(2,128)S(1)} %get-tuple-element.23), channel_id=1, source_target_pairs={{0,508},{4,0},{8,4},{12,8},{16,12},{20,16},{24,20},{28,24},{32,28}... | collective-permute-start | bytes 18440 | tf_op jit(solution)/shard_map/ppermute | solution.py:23
  87.7 15.8 %collective-permute-start.11 = (bf16[768,2,128]{2,0,1:T(8,128)(2,1)S(1)}, bf16[768,2,128]{2,0,1:T(8,128)(2,1)S(1)}, u32[]{:S(2)}, u32[]{:S(2)}) collective-permute-start(bf16[768,2,128]{2,0,1:T(8,128)(2,1)S(1)} %collective-permute-done.7), channel_id=1, source_target_pairs={{4,0},{8,4},{12,8},{16,12},{20,16},{24,20},{28,24},{32,28},{36,32}... | collective-permute-start | bytes 1179656 | tf_op jit(solution)/shard_map/ppermute | solution.py:17
  89.7 30.6 %collective-permute-start.15 = (f32[2,768]{1,0:T(2,128)S(1)}, f32[2,768]{1,0:T(2,128)S(1)}, u32[]{:S(2)}, u32[]{:S(2)}) collective-permute-start(f32[2,768]{1,0:T(2,128)S(1)} %get-tuple-element.12), channel_id=1, source_target_pairs={{0,508},{4,0},{8,4},{12,8},{16,12},{20,16},{24,20},{28,24},{32,28}... | collective-permute-start | bytes 18440 | tf_op jit(solution)/shard_map/ppermute | solution.py:23
  92.6 24.7 %collective-permute-start.4 = (f32[2,768,128]{2,1,0:T(8,128)S(1)}, f32[2,768,128]{2,1,0:T(8,128)S(1)}, u32[]{:S(2)}, u32[]{:S(2)}) collective-permute-start(f32[2,768,128]{2,1,0:T(8,128)S(1)} %multiply_add_fusion.1), channel_id=1, source_target_pairs={{0,508},{4,0},{8,4},{12,8},{16,12},{20,16},{24,20},{28,24},{32,28}... | collective-permute-start | bytes 2359304 | tf_op jit(solution)/shard_map/ppermute | solution.py:23
  118.3 19.9 %collective-permute-start.8 = (f32[2,768,128]{2,1,0:T(8,128)S(1)}, f32[2,768,128]{2,1,0:T(8,128)S(1)}, u32[]{:S(2)}, u32[]{:S(2)}) collective-permute-start(f32[2,768,128]{2,1,0:T(8,128)S(1)} %multiply_add_fusion), channel_id=1, source_target_pairs={{0,508},{4,0},{8,4},{12,8},{16,12},{20,16},{24,20},{28,24},{32,28}... | collective-permute-start | bytes 2359304 | tf_op jit(solution)/shard_map/ppermute | solution.py:23
  139.3 85.0 %collective-permute-start.12 = (bf16[2,768,128]{2,1,0:T(8,128)(2,1)S(1)}, bf16[2,768,128]{2,1,0:T(8,128)(2,1)S(1)}, u32[]{:S(2)}, u32[]{:S(2)}) collective-permute-start(bf16[2,768,128]{2,1,0:T(8,128)(2,1)S(1)} %add_convert_fusion), channel_id=1, source_target_pairs={{0,12},{4,16},{8,20},{12,24},{16,28},{20,32},{24,36},{28,40},{32,4... | collective-permute-start | bytes 1179656 | tf_op jit(solution)/shard_map/ppermute | solution.py:23
  145.6 73.6 %collective-permute-start.16 = (bf16[2,768]{1,0:T(2,128)(2,1)S(1)}, bf16[2,768]{1,0:T(2,128)(2,1)S(1)}, u32[]{:S(2)}, u32[]{:S(2)}) collective-permute-start(bf16[2,768]{1,0:T(2,128)(2,1)S(1)} %get-tuple-element.8), channel_id=1, source_target_pairs={{0,12},{4,16},{8,20},{12,24},{16,28},{20,32},{24,36},{28,40},{32,4... | collective-permute-start | bytes 9224 | tf_op jit(solution)/shard_map/ppermute | solution.py:23
  217.4 6.4 %collective-permute-start.17 = (bf16[2,768]{1,0:T(2,128)(2,1)S(1)}, bf16[2,768]{1,0:T(2,128)(2,1)S(1)}, u32[]{:S(2)}, u32[]{:S(2)}) collective-permute-start(bf16[2,768]{1,0:T(2,128)(2,1)S(1)} %get-tuple-element.4), channel_id=1, source_target_pairs={{0,12},{4,16},{8,20},{12,24},{16,28},{20,32},{24,36},{28,40},{32,4... | collective-permute-start | bytes 9224 | tf_op jit(solution)/shard_map/ppermute | solution.py:23
where the time goes:
time: 226 us
  starting transfers between devices  123 us (54%)
  waiting for transfers between devices  68.6 us (30%)
  matrix products  14.3 us (6%)
  other arithmetic  8.67 us (4%)
  blocking collectives  7.55 us (3%)
    ppermute x15, starting transfers between devices, from_behind(): return lax.ppermute(value, axis, pairs)  114 us
    ppermute x15, waiting for transfers between devices, from_behind(): return lax.ppermute(value, axis, pairs)  40.5 us
    ppermute x3, waiting for transfers between devices, passed_along(): lax.ppermute(value, axis, [(source, source + steps) for source in range(f...  28.2 us
    ppermute x3, starting transfers between devices, passed_along(): lax.ppermute(value, axis, [(source, source + steps) for source in range(f...  9.42 us
    dot_general x12, matrix products, attend_piece(): jnp.einsum('hqk,kd->hqd', weights.astype(jnp.bfloat16), values, preferred...  8.81 us
    all_gather x1, blocking collectives, per_device(): pieces = lax.all_gather(keys_values, 'hd', axis=1, tiled=True)  7.55 us
    dot_general x12, matrix products, attend_piece(): jnp.einsum('qhd,kd->hqk', queries, key_rows, preferred_element_type=jnp.f...  5.51 us
  transfers between devices with their start and end apart: 18, of which 8 were waited for; matrix products, arithmetic and copies ran while one was open for 10% of the time, Pallas kernels for 0%

commit v1 on v0

v1 whole, which is shorter than its diff:
```python
import functools
import math

import jax
import jax.numpy as jnp
from jax import lax
from jax.experimental import pallas as pl
from jax.experimental.pallas import tpu as pltpu
from jax.sharding import Mesh, PartitionSpec as P

GROUP = 4
MASKED_SCORE = -1e30
LOG2E = math.log2(math.e)
LANES = 128


def rows_of(block, tokens, heads):
    return pl.ds(block * tokens * heads, tokens * heads)


def start_columns(starts_ref, cols_ref, heads):
    for j in range(starts_ref.shape[0]):
        row = starts_ref[j : j + 1, :].astype(jnp.float32)
        tall = jnp.transpose(jnp.broadcast_to(row, (LANES, LANES)))
        for h in range(heads):
            cols_ref[pl.ds(j * LANES * heads + h, LANES, stride=heads), :] = tall


def scores_of(q, keys):
    return lax.dot_general(q, keys, (((1,), (1,)), ((), ())), preferred_element_type=jnp.float32)


def with_ones(values):
    return jnp.concatenate([values, jnp.ones_like(values)], axis=1)


def mix(weights, values):
    return lax.dot_general(
        weights.astype(jnp.bfloat16), values, (((1,), (0,)), ((), ())), preferred_element_type=jnp.float32
    )


def own_kernel(heads, tokens, scale, meta_ref, starts_ref, q_ref, kv_ref, peak_ref, acc_ref, cols_ref):
    start_columns(starts_ref, cols_ref, heads)
    factor = scale * LOG2E
    base = meta_ref[0].astype(jnp.float32)
    pieces = kv_ref.shape[0]
    keys = jnp.concatenate([kv_ref[i, 0] for i in range(pieces)], axis=0)
    values = with_ones(jnp.concatenate([kv_ref[i, 1] for i in range(pieces)], axis=0))
    blocks = q_ref.shape[0] // (tokens * heads)
    for i in range(blocks):
        rows = rows_of(i, tokens, heads)
        width = (i + 1) * tokens
        s = scores_of(q_ref[rows, :], keys[:width])
        shape = s.shape
        k_pos = lax.broadcasted_iota(jnp.int32, shape, 1)
        q_pos = i * tokens + lax.broadcasted_iota(jnp.int32, shape, 0) // heads
        cols = jnp.concatenate([cols_ref[rows, :] - base] * (width // LANES), axis=1)
        visible = (k_pos <= q_pos) & (k_pos.astype(jnp.float32) >= cols)
        s = jnp.where(visible, s, MASKED_SCORE)
        peak = jnp.max(s, axis=1, keepdims=True)
        weights = jnp.exp2((s - peak) * factor)
        peak_ref[rows, :] = jnp.broadcast_to(peak, (tokens * heads, LANES))
        acc_ref[rows, :] = mix(weights, values[:width])


def earlier_kernel(
    heads, tokens, scale, meta_ref, firsts_ref, starts_ref, q_ref, far_ref, near_ref, peak_in, acc_in,
    out_ref, log_ref, peak_ref, acc_ref, cols_ref,
):
    start_columns(starts_ref, cols_ref, heads)
    factor = scale * LOG2E
    count = q_ref.shape[0]
    blocks = count // (tokens * heads)
    span = count // heads
    peak_ref[...] = peak_in[...]
    acc_ref[...] = acc_in[...]

    def pieces_of(which, half):
        if which == 1:
            return [near_ref[0, i, half] for i in range(4)]
        if which == 3:
            return [near_ref[1, i, half] for i in range(4)]
        return [far_ref[c, i, half] for c in range(2) for i in range(2)]

    for distance in (1, 2, 3):
        first = meta_ref[0] - distance * span

        def attend(i, masked, distance=distance, first=first):
            keys = jnp.concatenate(pieces_of(distance, 0), axis=0)
            values = with_ones(jnp.concatenate(pieces_of(distance, 1), axis=0))
            rows = rows_of(i, tokens, heads)
            s = scores_of(q_ref[rows, :], keys)
            if masked:
                k_pos = lax.broadcasted_iota(jnp.int32, s.shape, 1).astype(jnp.float32)
                cols = cols_ref[rows, :] - first.astype(jnp.float32)
                cols = jnp.concatenate([cols] * (s.shape[1] // LANES), axis=1)
                s = jnp.where(k_pos >= cols, s, MASKED_SCORE)
            before = peak_ref[rows, :1]
            peak = jnp.maximum(before, jnp.max(s, axis=1, keepdims=True))
            weights = jnp.exp2((s - peak) * factor)
            fade = jnp.exp2((before - peak) * factor)
            peak_ref[rows, :] = jnp.broadcast_to(peak, (tokens * heads, LANES))
            acc_ref[rows, :] = acc_ref[rows, :] * fade + mix(weights, values)

        for i in range(blocks):
            lowest = firsts_ref[i * tokens]
            highest = firsts_ref[(i + 1) * tokens - 1]
            some = lowest < first + span
            clear = highest <= first
            pl.when(clear)(functools.partial(attend, i, False))
            pl.when(some & jnp.logical_not(clear))(functools.partial(attend, i, True))

    total = acc_ref[:, LANES:]
    out_ref[...] = (acc_ref[:, :LANES] / total).astype(out_ref.dtype)
    cols_ref[...] = peak_ref[...] * scale + jnp.log(total)
    eye = lax.broadcasted_iota(jnp.int32, (LANES, LANES), 0) == lax.broadcasted_iota(jnp.int32, (LANES, LANES), 1)
    for h in range(heads):
        for j in range(span // LANES):
            tall = cols_ref[pl.ds(j * LANES * heads + h, LANES, stride=heads), :]
            log_ref[h : h + 1, j * LANES : (j + 1) * LANES] = jnp.sum(
                jnp.where(eye, tall, 0.0), axis=0, keepdims=True
            )


def place(s, z, c):
    return (s * 2 + z) * 2 + c


def permuted(value, source):
    pairs = []
    for s in range(GROUP):
        for z in range(2):
            for c in range(2):
                at = source(s, z, c)
                if at[0] >= 0:
                    pairs.append((place(*at), place(s, z, c)))
    return lax.ppermute(value, ("s", "z", "c"), pairs)


def per_device(queries, keys_values, doc_start):
    span, heads, width = queries.shape
    count = span * heads
    scale = width ** (-0.5)
    tokens = 128
    shard = lax.axis_index("g") * GROUP + lax.axis_index("s")
    meta = (shard * span).astype(jnp.int32).reshape(1)
    flat_q = queries.reshape(count, width)
    starts = doc_start.reshape(span // LANES, LANES)

    own = lax.all_gather(keys_values, ("z", "c"), axis=0)
    half = lax.dynamic_slice_in_dim(own, lax.axis_index("c") * 2, 2, 0)
    near = permuted(own, lambda s, z, c: (s - 1, z, c) if c == 0 else (s - 3, z, c))
    far = permuted(half, lambda s, z, c: (s - 2, z, c))

    smem = pl.BlockSpec(memory_space=pltpu.SMEM)
    vmem = pl.BlockSpec(memory_space=pltpu.VMEM)
    peak, acc = pl.pallas_call(
        functools.partial(own_kernel, heads, tokens, scale),
        out_shape=(
            jax.ShapeDtypeStruct((count, LANES), jnp.float32),
            jax.ShapeDtypeStruct((count, 2 * width), jnp.float32),
        ),
        in_specs=[smem, vmem, vmem, vmem],
        out_specs=(vmem, vmem),
        scratch_shapes=[pltpu.VMEM((count, LANES), jnp.float32)],
        compiler_params=pltpu.CompilerParams(vmem_limit_bytes=32 * 1024 * 1024),
        cost_estimate=pl.CostEstimate(flops=600_000_000, bytes_accessed=4_000_000, transcendentals=700_000),
    )(meta, starts, flat_q, own)

    near = lax.all_gather(near, "c", axis=0)
    far = lax.all_gather(far, "c", axis=0)
    out, log_total = pl.pallas_call(
        functools.partial(earlier_kernel, heads, tokens, scale),
        out_shape=(
            jax.ShapeDtypeStruct((count, width), jnp.bfloat16),
            jax.ShapeDtypeStruct((heads, span), jnp.float32),
        ),
        in_specs=[smem, smem, vmem, vmem, vmem, vmem, vmem, vmem],
        out_specs=(vmem, vmem),
        scratch_shapes=[
            pltpu.VMEM((count, LANES), jnp.float32),
            pltpu.VMEM((count, 2 * width), jnp.float32),
            pltpu.VMEM((count, LANES), jnp.float32),
        ],
        compiler_params=pltpu.CompilerParams(vmem_limit_bytes=32 * 1024 * 1024),
        cost_estimate=pl.CostEstimate(flops=4_000_000_000, bytes_accessed=6_000_000, transcendentals=4_000_000),
    )(meta, doc_start, starts, flat_q, far, near, peak, acc)
    return out.reshape(span, heads, width), log_total


def solution(mesh):
    grid = mesh.devices.reshape(-1, GROUP, 2, 2)
    return jax.shard_map(
        per_device,
        mesh=Mesh(grid, ("g", "s", "z", "c")),
        in_specs=(P(("g", "s"), ("z", "c"), None), P(None, ("g", "s", "z", "c"), None), P(("g", "s"))),
        out_specs=(P(("g", "s"), ("z", "c"), None), P(("z", "c"), ("g", "s"))),
        check_vma=False,
    )
```

time: 226 us -> 42.5 us (0.19)
  the two profiles are of different devices: /device:TPU:178 before, /device:TPU:47 now
where the time goes in v1:
time: 42.5 us; the launch traced here: 42.3 us
  Pallas kernels  19.2 us (45%)
  blocking collectives  13.2 us (31%)
  waiting for transfers between devices  5.01 us (12%)
  starting transfers between devices  2.57 us (6%)
  local copies, waits for them, and re-layouts  1.7 us (4%)
  between operations  0.69 us (2%)
    pallas_call x1, Pallas kernels, per_device(): pl.pallas_call(functools.partial(earlier_kernel, heads, tokens, scale), o...  17.3 us
    all_gather x1, blocking collectives, per_device(): own = lax.all_gather(keys_values, ('z', 'c'), axis=0)  8.06 us
    ppermute x2, waiting for transfers between devices, permuted(): return lax.ppermute(value, ('s', 'z', 'c'), pairs)  5.01 us
    all_gather x1, blocking collectives, per_device(): far = lax.all_gather(far, 'c', axis=0)  2.73 us
    ppermute x2, starting transfers between devices, permuted(): return lax.ppermute(value, ('s', 'z', 'c'), pairs)  2.57 us
    all_gather x1, blocking collectives, per_device(): near = lax.all_gather(near, 'c', axis=0)  2.36 us
    pallas_call x1, Pallas kernels, per_device(): pl.pallas_call(functools.partial(own_kernel, heads, tokens, scale), out_s...  1.86 us
    unnamed x4, local copies, waits for them, and re-layouts  1.68 us
  transfers between devices with their start and end apart: 2, of which 2 were waited for; matrix products, arithmetic and copies ran while one was open for 0% of the time, Pallas kernels for 4%

profile of v1, /device:TPU:47, one launch (start us, length us, event | category | flops | bytes accessed | tf_op | source)
XLA Modules:
  0.0 42.3 jit_solution(3826317966426560696)
XLA Ops:
  0.6 8.1 %all-gather = bf16[8,192,128]{2,1,0:T(8,128)(2,1)S(1)} all-gather(bf16[2,192,128]{2,1,0:T(8,128)(2,1)} %param.4), channel_id=2, replica_groups=mesh['g'=32,'s'=4,'z'=2,'c'=2] {'z','c'}, dimensions={0}, use_global_device_ids=true | all-gather | bytes 491520 | tf_op jit(solution)/shard_map/all_gather | solution.py:151
  8.7 1.3 %collective-permute-start.1 = (bf16[4,2,192,128]{3,2,1,0:T(8,128)(2,1)S(1)}, bf16[4,2,192,128]{3,2,1,0:T(8,128)(2,1)S(1)}, u32[]{:S(2)}, u32[]{:S(2)}) collective-permute-start(bf16[4,2,192,128]{3,2,1,0:T(8,128)(2,1)S(1)} %bitcast.7), channel_id=1, source_target_pairs={{0,4},{2,6},{4,8},{6,10},{8,12},{1,13},{10,14},{3,15},{16,20},{18,... | collective-permute-start | bytes 1179656 | tf_op jit(solution)/shard_map/ppermute | solution.py:138
  10.0 1.3 %collective-permute-start = (bf16[2,2,192,128]{3,2,1,0:T(8,128)(2,1)S(1)}, bf16[2,2,192,128]{3,2,1,0:T(8,128)(2,1)S(1)}, u32[]{:S(2)}, u32[]{:S(2)}) collective-permute-start(bf16[2,2,192,128]{3,2,1,0:T(8,128)(2,1)S(1)} %constant_dynamic-slice_fusion), channel_id=1, source_target_pairs={{0,8},{1,9},{2,10},{3,11},{4,12},{5,13},{6,14},{7,15},{16,24},{17,... | collective-permute-start | bytes 589832 | tf_op jit(solution)/shard_map/ppermute | solution.py:138
  11.3 0.0 copy-start
  11.3 1.0 %copy-done = bf16[768,2,128]{2,1,0:T(2,128)(2,1)S(1)} copy-done((bf16[768,2,128]{2,1,0:T(2,128)(2,1)S(1)}, bf16[768,2,128]{2,1,0:T(2,128)(2,1)}, u32[]{:S(2)}) %copy-start) | copy-done | bytes 393240
  12.3 0.0 copy-start.1
  12.3 0.7 %copy-done.1 = s32[768]{0:T(1024)S(1)} copy-done((s32[768]{0:T(1024)S(1)}, s32[768]{0:T(1024)}, u32[]{:S(2)}) %copy-start.1) | copy-done | bytes 3096
  13.0 1.9 %shard_map.50 = (f32[1536,128]{1,0:T(8,128)S(1)}, f32[1536,256]{1,0:T(8,128)S(1)}) custom-call(s32[1]{0:T(128)} %bitcast.meta_ref, s32[6,128]{1,0:T(8,128)S(1)} %bitcast.14, bf16[1536,128]{1,0:T(8,128)(2,1)S(1)} %bitcast.12, bf16[4,2,192,128]{3,2,1,0:T(8,128)(2,1)S(1)} %bitcast.9), custom_call_target="tpu_custom_call" | custom-call | flops 600000000 | bytes 4000000 | tf_op jit(solution)/shard_map/pallas_call | solution.py:158
  14.9 4.9 %collective-permute-done = bf16[2,2,192,128]{3,2,1,0:T(8,128)(2,1)S(1)} collective-permute-done((bf16[2,2,192,128]{3,2,1,0:T(8,128)(2,1)S(1)}, bf16[2,2,192,128]{3,2,1,0:T(8,128)(2,1)S(1)}, u32[]{:S(2)}, u32[]{:S(2)}) %collective-permute-start) | collective-permute-done | bytes 196640 | tf_op jit(solution)/shard_map/ppermute | solution.py:138
  19.8 2.7 %all-gather.1 = bf16[4,2,192,128]{3,2,1,0:T(8,128)(2,1)S(1)} all-gather(bf16[2,2,192,128]{3,2,1,0:T(8,128)(2,1)S(1)} %collective-permute-done), channel_id=3, replica_groups=mesh['g'=32,'s'=4,'z'=2,'c'=2] {'c'}, dimensions={0}, use_global_device_ids=true | all-gather | bytes 589824 | tf_op jit(solution)/shard_map/all_gather | solution.py:172
  22.5 0.1 collective-permute-done.1
  22.6 2.4 %all-gather.2 = bf16[8,2,192,128]{3,2,1,0:T(8,128)(2,1)S(1)} all-gather(bf16[4,2,192,128]{3,2,1,0:T(8,128)(2,1)S(1)} %collective-permute-done.1), channel_id=4, replica_groups=mesh['g'=32,'s'=4,'z'=2,'c'=2] {'c'}, dimensions={0}, use_global_device_ids=true | all-gather | bytes 1179648 | tf_op jit(solution)/shard_map/all_gather | solution.py:171
  25.0 17.3 %shard_map.51 = (bf16[1536,128]{1,0:T(8,128)(2,1)}, f32[2,768]{1,0:T(2,128)}) custom-call(s32[1]{0:T(128)} %bitcast.meta_ref, s32[768]{0:T(1024)S(1)} %copy-done.1, s32[6,128]{1,0:T(8,128)S(1)} %bitcast.15, bf16[1536,128]{1,0:T(8,128)(2,1)S(1)} %bitcast.13, bf16[2,2,2,192,128]{4,3,2,1,0:T(8,128)(2,1)S(1)} %bitcast.11, ...), custom_call_target="tpu_custom_call" | custom-call | flops 4000000000 | bytes 6000000 | tf_op jit(solution)/shard_map/pallas_call | solution.py:173
  (1 shorter events, 0.0 us)
Async XLA Ops:
  8.7 13.9 %collective-permute-start.1 = (bf16[4,2,192,128]{3,2,1,0:T(8,128)(2,1)S(1)}, bf16[4,2,192,128]{3,2,1,0:T(8,128)(2,1)S(1)}, u32[]{:S(2)}, u32[]{:S(2)}) collective-permute-start(bf16[4,2,192,128]{3,2,1,0:T(8,128)(2,1)S(1)} %bitcast.7), channel_id=1, source_target_pairs={{0,4},{2,6},{4,8},{6,10},{8,12},{1,13},{10,14},{3,15},{16,20},{18,... | collective-permute-start | bytes 1179656 | tf_op jit(solution)/shard_map/ppermute | solution.py:138
  10.0 9.8 %collective-permute-start = (bf16[2,2,192,128]{3,2,1,0:T(8,128)(2,1)S(1)}, bf16[2,2,192,128]{3,2,1,0:T(8,128)(2,1)S(1)}, u32[]{:S(2)}, u32[]{:S(2)}) collective-permute-start(bf16[2,2,192,128]{3,2,1,0:T(8,128)(2,1)S(1)} %constant_dynamic-slice_fusion), channel_id=1, source_target_pairs={{0,8},{1,9},{2,10},{3,11},{4,12},{5,13},{6,14},{7,15},{16,24},{17,... | collective-permute-start | bytes 589832 | tf_op jit(solution)/shard_map/ppermute | solution.py:138
  11.3 1.0 %copy-start = (bf16[768,2,128]{2,1,0:T(2,128)(2,1)S(1)}, bf16[768,2,128]{2,1,0:T(2,128)(2,1)}, u32[]{:S(2)}) copy-start(bf16[768,2,128]{2,1,0:T(2,128)(2,1)} %param.3) | copy-start | bytes 1179652
  12.3 0.7 %copy-start.1 = (s32[768]{0:T(1024)S(1)}, s32[768]{0:T(1024)}, u32[]{:S(2)}) copy-start(s32[768]{0:T(1024)} %firsts_ref.1) | copy-start | bytes 9220

commit v2 on v1

--- a/solution.py
+++ b/solution.py
@@ -64,17 +64,32 @@
         acc_ref[rows, :] = mix(weights, values[:width])
 
 
+def merge(rows_total, block, peak_ref, acc_ref, q_ref, keys, values, seen_rows, seen_keys, factor):
+    values = with_ones(values)
+    for i in range(rows_total // block):
+        rows = pl.ds(i * block, block)
+        s = scores_of(q_ref[rows, :], keys)
+        if seen_keys is not None:
+            s = jnp.where(seen_keys, s, MASKED_SCORE)
+        seen = i * block + lax.broadcasted_iota(jnp.int32, (block, 1), 0) < seen_rows
+        before = peak_ref[rows, :1]
+        peak = jnp.where(seen, jnp.maximum(before, jnp.max(s, axis=1, keepdims=True)), before)
+        weights = jnp.exp2((s - jnp.where(seen, peak, -MASKED_SCORE)) * factor)
+        fade = jnp.exp2((before - peak) * factor)
+        peak_ref[rows, :] = jnp.broadcast_to(peak, (block, LANES))
+        acc_ref[rows, :] = acc_ref[rows, :] * fade + mix(weights, values)
+
+
 def earlier_kernel(
-    heads, tokens, scale, meta_ref, firsts_ref, starts_ref, q_ref, far_ref, near_ref, peak_in, acc_in,
+    heads, block, scale, meta_ref, firsts_ref, starts_ref, q_ref, far_ref, near_ref, peak_in, acc_in,
     out_ref, log_ref, peak_ref, acc_ref, cols_ref,
 ):
-    start_columns(starts_ref, cols_ref, heads)
+    del peak_in, acc_in
     factor = scale * LOG2E
     count = q_ref.shape[0]
-    blocks = count // (tokens * heads)
     span = count // heads
-    peak_ref[...] = peak_in[...]
-    acc_ref[...] = acc_in[...]
+    begin = firsts_ref[0]
+    seen_rows = jnp.sum(jnp.where(starts_ref[...] == begin, 1.0, 0.0)).astype(jnp.int32) * heads
 
     def pieces_of(which, half):
         if which == 1:
@@ -86,30 +101,14 @@
     for distance in (1, 2, 3):
         first = meta_ref[0] - distance * span
 
-        def attend(i, masked, distance=distance, first=first):
+        def attend(cut, distance=distance, first=first):
             keys = jnp.concatenate(pieces_of(distance, 0), axis=0)
-            values = with_ones(jnp.concatenate(pieces_of(distance, 1), axis=0))
-            rows = rows_of(i, tokens, heads)
-            s = scores_of(q_ref[rows, :], keys)
-            if masked:
-                k_pos = lax.broadcasted_iota(jnp.int32, s.shape, 1).astype(jnp.float32)
-                cols = cols_ref[rows, :] - first.astype(jnp.float32)
-                cols = jnp.concatenate([cols] * (s.shape[1] // LANES), axis=1)
-                s = jnp.where(k_pos >= cols, s, MASKED_SCORE)
-            before = peak_ref[rows, :1]
-            peak = jnp.maximum(before, jnp.max(s, axis=1, keepdims=True))
-            weights = jnp.exp2((s - peak) * factor)
-            fade = jnp.exp2((before - peak) * factor)
-            peak_ref[rows, :] = jnp.broadcast_to(peak, (tokens * heads, LANES))
-            acc_ref[rows, :] = acc_ref[rows, :] * fade + mix(weights, values)
+            values = jnp.concatenate(pieces_of(distance, 1), axis=0)
+            seen_keys = first + lax.broadcasted_iota(jnp.int32, (1, span), 1) >= begin if cut else None
+            merge(count, block, peak_ref, acc_ref, q_ref, keys, values, seen_rows, seen_keys, factor)
 
-        for i in range(blocks):
-            lowest = firsts_ref[i * tokens]
-            highest = firsts_ref[(i + 1) * tokens - 1]
-            some = lowest < first + span
-            clear = highest <= first
-            pl.when(clear)(functools.partial(attend, i, False))
-            pl.when(some & jnp.logical_not(clear))(functools.partial(attend, i, True))
+        pl.when(begin <= first)(functools.partial(attend, False))
+        pl.when((begin > first) & (begin < first + span))(functools.partial(attend, True))
 
     total = acc_ref[:, LANES:]
     out_ref[...] = (acc_ref[:, :LANES] / total).astype(out_ref.dtype)
@@ -170,19 +169,18 @@
 
     near = lax.all_gather(near, "c", axis=0)
     far = lax.all_gather(far, "c", axis=0)
-    out, log_total = pl.pallas_call(
-        functools.partial(earlier_kernel, heads, tokens, scale),
+    out, log_total, _, _ = pl.pallas_call(
+        functools.partial(earlier_kernel, heads, 256, scale),
         out_shape=(
             jax.ShapeDtypeStruct((count, width), jnp.bfloat16),
             jax.ShapeDtypeStruct((heads, span), jnp.float32),
+            jax.ShapeDtypeStruct((count, LANES), jnp.float32),
+            jax.ShapeDtypeStruct((count, 2 * width), jnp.float32),
         ),
         in_specs=[smem, smem, vmem, vmem, vmem, vmem, vmem, vmem],
-        out_specs=(vmem, vmem),
-        scratch_shapes=[
-            pltpu.VMEM((count, LANES), jnp.float32),
-            pltpu.VMEM((count, 2 * width), jnp.float32),
-            pltpu.VMEM((count, LANES), jnp.float32),
-        ],
+        out_specs=(vmem, vmem, vmem, vmem),
+        input_output_aliases={6: 2, 7: 3},
+        scratch_shapes=[pltpu.VMEM((count, LANES), jnp.float32)],
         compiler_params=pltpu.CompilerParams(vmem_limit_bytes=32 * 1024 * 1024),
         cost_estimate=pl.CostEstimate(flops=4_000_000_000, bytes_accessed=6_000_000, transcendentals=4_000_000),
     )(meta, doc_start, starts, flat_q, far, near, peak, acc)

time: 42.5 us -> 35.6 us (0.84)
  the two profiles are of different devices: /device:TPU:47 before, /device:TPU:5 now
where the time goes in v2:
time: 35.6 us; the launch traced here: 35.4 us
  blocking collectives  16 us (45%)
  Pallas kernels  8.39 us (24%)
  waiting for transfers between devices  6.61 us (19%)
  starting transfers between devices  1.97 us (6%)
  local copies, waits for them, and re-layouts  1.7 us (5%)
  between operations  0.69 us (2%)
    all_gather x1, blocking collectives, per_device(): own = lax.all_gather(keys_values, ('z', 'c'), axis=0)  8.06 us
    ppermute x2, waiting for transfers between devices, permuted(): return lax.ppermute(value, ('s', 'z', 'c'), pairs)  6.61 us
    pallas_call x1, Pallas kernels, per_device(): pl.pallas_call(functools.partial(earlier_kernel, heads, 256, scale), out_...  6.53 us
    all_gather x1, blocking collectives, per_device(): far = lax.all_gather(far, 'c', axis=0)  5.6 us
    all_gather x1, blocking collectives, per_device(): near = lax.all_gather(near, 'c', axis=0)  2.36 us
    ppermute x2, starting transfers between devices, permuted(): return lax.ppermute(value, ('s', 'z', 'c'), pairs)  1.97 us
    pallas_call x1, Pallas kernels, per_device(): pl.pallas_call(functools.partial(own_kernel, heads, tokens, scale), out_s...  1.87 us
    unnamed x4, local copies, waits for them, and re-layouts  1.68 us
  transfers between devices with their start and end apart: 2, of which 1 were waited for; matrix products, arithmetic and copies ran while one was open for 0% of the time, Pallas kernels for 5%

profile of v2, /device:TPU:5, one launch (start us, length us, event | category | flops | bytes accessed | tf_op | source)
XLA Modules:
  0.0 35.4 jit_solution(411208378017782145)
XLA Ops:
  0.6 8.1 %all-gather = bf16[8,192,128]{2,1,0:T(8,128)(2,1)S(1)} all-gather(bf16[2,192,128]{2,1,0:T(8,128)(2,1)} %param.4), channel_id=2, replica_groups=mesh['g'=32,'s'=4,'z'=2,'c'=2] {'z','c'}, dimensions={0}, use_global_device_ids=true | all-gather | bytes 491520 | tf_op jit(solution)/shard_map/all_gather | solution.py:150
  8.7 0.7 %collective-permute-start.1 = (bf16[4,2,192,128]{3,2,1,0:T(8,128)(2,1)S(1)}, bf16[4,2,192,128]{3,2,1,0:T(8,128)(2,1)S(1)}, u32[]{:S(2)}, u32[]{:S(2)}) collective-permute-start(bf16[4,2,192,128]{3,2,1,0:T(8,128)(2,1)S(1)} %bitcast.7), channel_id=1, source_target_pairs={{0,4},{2,6},{4,8},{6,10},{8,12},{1,13},{10,14},{3,15},{16,20},{18,... | collective-permute-start | bytes 1179656 | tf_op jit(solution)/shard_map/ppermute | solution.py:137
  9.4 1.3 %collective-permute-start = (bf16[2,2,192,128]{3,2,1,0:T(8,128)(2,1)S(1)}, bf16[2,2,192,128]{3,2,1,0:T(8,128)(2,1)S(1)}, u32[]{:S(2)}, u32[]{:S(2)}) collective-permute-start(bf16[2,2,192,128]{3,2,1,0:T(8,128)(2,1)S(1)} %constant_dynamic-slice_fusion), channel_id=1, source_target_pairs={{0,8},{1,9},{2,10},{3,11},{4,12},{5,13},{6,14},{7,15},{16,24},{17,... | collective-permute-start | bytes 589832 | tf_op jit(solution)/shard_map/ppermute | solution.py:137
  10.7 0.0 copy-start
  10.7 1.0 %copy-done = bf16[768,2,128]{2,1,0:T(2,128)(2,1)S(1)} copy-done((bf16[768,2,128]{2,1,0:T(2,128)(2,1)S(1)}, bf16[768,2,128]{2,1,0:T(2,128)(2,1)}, u32[]{:S(2)}) %copy-start) | copy-done | bytes 393240
  11.7 0.0 copy-start.1
  11.7 0.7 %copy-done.1 = s32[768]{0:T(1024)S(1)} copy-done((s32[768]{0:T(1024)S(1)}, s32[768]{0:T(1024)}, u32[]{:S(2)}) %copy-start.1) | copy-done | bytes 3096
  12.4 1.9 %shard_map.50 = (f32[1536,128]{1,0:T(8,128)S(1)}, f32[1536,256]{1,0:T(8,128)S(1)}) custom-call(s32[1]{0:T(128)} %bitcast.meta_ref, s32[6,128]{1,0:T(8,128)S(1)} %bitcast.14, bf16[1536,128]{1,0:T(8,128)(2,1)S(1)} %bitcast.12, bf16[4,2,192,128]{3,2,1,0:T(8,128)(2,1)S(1)} %bitcast.9), custom_call_target="tpu_custom_call" | custom-call | flops 600000000 | bytes 4000000 | tf_op jit(solution)/shard_map/pallas_call | solution.py:157
  14.3 6.6 %collective-permute-done = bf16[2,2,192,128]{3,2,1,0:T(8,128)(2,1)S(1)} collective-permute-done((bf16[2,2,192,128]{3,2,1,0:T(8,128)(2,1)S(1)}, bf16[2,2,192,128]{3,2,1,0:T(8,128)(2,1)S(1)}, u32[]{:S(2)}, u32[]{:S(2)}) %collective-permute-start) | collective-permute-done | bytes 196640 | tf_op jit(solution)/shard_map/ppermute | solution.py:137
  20.9 5.6 %all-gather.1 = bf16[4,2,192,128]{3,2,1,0:T(8,128)(2,1)S(1)} all-gather(bf16[2,2,192,128]{3,2,1,0:T(8,128)(2,1)S(1)} %collective-permute-done), channel_id=3, replica_groups=mesh['g'=32,'s'=4,'z'=2,'c'=2] {'c'}, dimensions={0}, use_global_device_ids=true | all-gather | bytes 589824 | tf_op jit(solution)/shard_map/all_gather | solution.py:171
  26.5 0.0 collective-permute-done.1
  26.5 2.4 %all-gather.2 = bf16[8,2,192,128]{3,2,1,0:T(8,128)(2,1)S(1)} all-gather(bf16[4,2,192,128]{3,2,1,0:T(8,128)(2,1)S(1)} %collective-permute-done.1), channel_id=4, replica_groups=mesh['g'=32,'s'=4,'z'=2,'c'=2] {'c'}, dimensions={0}, use_global_device_ids=true | all-gather | bytes 1179648 | tf_op jit(solution)/shard_map/all_gather | solution.py:170
  28.8 6.5 %shard_map.51 = (bf16[1536,128]{1,0:T(8,128)(2,1)}, f32[2,768]{1,0:T(2,128)}, f32[1536,128]{1,0:T(8,128)S(1)}, f32[1536,256]{1,0:T(8,128)S(1)}) custom-call(s32[1]{0:T(128)} %bitcast.meta_ref, s32[768]{0:T(1024)S(1)} %copy-done.1, s32[6,128]{1,0:T(8,128)S(1)} %bitcast.15, ...), custom_call_target="tpu_custom_call", output_to_operand_aliasing={{2}: (6, {}), {3}: (7, {})} | custom-call | flops 4000000000 | bytes 6000000 | tf_op jit(solution)/shard_map/pallas_call | solution.py:172
  (1 shorter events, 0.0 us)
Async XLA Ops:
  8.7 17.8 %collective-permute-start.1 = (bf16[4,2,192,128]{3,2,1,0:T(8,128)(2,1)S(1)}, bf16[4,2,192,128]{3,2,1,0:T(8,128)(2,1)S(1)}, u32[]{:S(2)}, u32[]{:S(2)}) collective-permute-start(bf16[4,2,192,128]{3,2,1,0:T(8,128)(2,1)S(1)} %bitcast.7), channel_id=1, source_target_pairs={{0,4},{2,6},{4,8},{6,10},{8,12},{1,13},{10,14},{3,15},{16,20},{18,... | collective-permute-start | bytes 1179656 | tf_op jit(solution)/shard_map/ppermute | solution.py:137
  9.4 11.5 %collective-permute-start = (bf16[2,2,192,128]{3,2,1,0:T(8,128)(2,1)S(1)}, bf16[2,2,192,128]{3,2,1,0:T(8,128)(2,1)S(1)}, u32[]{:S(2)}, u32[]{:S(2)}) collective-permute-start(bf16[2,2,192,128]{3,2,1,0:T(8,128)(2,1)S(1)} %constant_dynamic-slice_fusion), channel_id=1, source_target_pairs={{0,8},{1,9},{2,10},{3,11},{4,12},{5,13},{6,14},{7,15},{16,24},{17,... | collective-permute-start | bytes 589832 | tf_op jit(solution)/shard_map/ppermute | solution.py:137
  10.7 1.0 %copy-start = (bf16[768,2,128]{2,1,0:T(2,128)(2,1)S(1)}, bf16[768,2,128]{2,1,0:T(2,128)(2,1)}, u32[]{:S(2)}) copy-start(bf16[768,2,128]{2,1,0:T(2,128)(2,1)} %param.3) | copy-start | bytes 1179652
  11.7 0.7 %copy-start.1 = (s32[768]{0:T(1024)S(1)}, s32[768]{0:T(1024)}, u32[]{:S(2)}) copy-start(s32[768]{0:T(1024)} %firsts_ref.1) | copy-start | bytes 9220

commit v3 on v2

v3 whole, which is shorter than its diff:
```python
import functools
import math

import jax
import jax.numpy as jnp
from jax import lax
from jax.experimental import pallas as pl
from jax.experimental.pallas import tpu as pltpu
from jax.sharding import Mesh, PartitionSpec as P

GROUP = 4
MASKED_SCORE = -1e30
LOG2E = math.log2(math.e)
LANES = 128


def rows_of(block, tokens, heads):
    return pl.ds(block * tokens * heads, tokens * heads)


def start_columns(starts_ref, cols_ref, heads):
    for j in range(starts_ref.shape[0]):
        row = starts_ref[j : j + 1, :].astype(jnp.float32)
        tall = jnp.transpose(jnp.broadcast_to(row, (LANES, LANES)))
        for h in range(heads):
            cols_ref[pl.ds(j * LANES * heads + h, LANES, stride=heads), :] = tall


def scores_of(q, keys):
    return lax.dot_general(q, keys, (((1,), (1,)), ((), ())), preferred_element_type=jnp.float32)


def with_ones(values):
    return jnp.concatenate([values, jnp.ones_like(values)], axis=1)


def mix(weights, values):
    return lax.dot_general(
        weights.astype(jnp.bfloat16), values, (((1,), (0,)), ((), ())), preferred_element_type=jnp.float32
    )


def own_kernel(heads, tokens, scale, meta_ref, starts_ref, q_ref, kv_ref, peak_ref, acc_ref, first_ref, cols_ref):
    begin = jnp.min(starts_ref[...].astype(jnp.float32))
    first_ref[0] = begin.astype(jnp.int32)
    first_ref[1] = jnp.sum(jnp.where(starts_ref[...].astype(jnp.float32) == begin, 1.0, 0.0)).astype(jnp.int32) * heads
    start_columns(starts_ref, cols_ref, heads)
    factor = scale * LOG2E
    base = meta_ref[0].astype(jnp.float32)
    pieces = kv_ref.shape[0]
    keys = jnp.concatenate([kv_ref[i, 0] for i in range(pieces)], axis=0)
    values = with_ones(jnp.concatenate([kv_ref[i, 1] for i in range(pieces)], axis=0))
    blocks = q_ref.shape[0] // (tokens * heads)
    for i in range(blocks):
        rows = rows_of(i, tokens, heads)
        width = (i + 1) * tokens
        s = scores_of(q_ref[rows, :], keys[:width])
        shape = s.shape
        k_pos = lax.broadcasted_iota(jnp.int32, shape, 1)
        q_pos = i * tokens + lax.broadcasted_iota(jnp.int32, shape, 0) // heads
        cols = jnp.concatenate([cols_ref[rows, :] - base] * (width // LANES), axis=1)
        visible = (k_pos <= q_pos) & (k_pos.astype(jnp.float32) >= cols)
        s = jnp.where(visible, s, MASKED_SCORE)
        peak = jnp.max(s, axis=1, keepdims=True)
        weights = jnp.exp2((s - peak) * factor)
        peak_ref[rows, :] = jnp.broadcast_to(peak, (tokens * heads, LANES))
        acc_ref[rows, :] = mix(weights, values[:width])


def block_sums(rows, block, peak_ref, acc_ref, q_ref, chunks, factor):
    q = q_ref[rows, :]
    before = peak_ref[rows, :1]
    peak = before
    met = []
    for keys, values, seen, seen_keys in chunks:
        s = scores_of(q, keys)
        if seen_keys is not None:
            s = jnp.where(seen_keys, s, MASKED_SCORE)
        peak = jnp.where(seen, jnp.maximum(peak, jnp.max(s, axis=1, keepdims=True)), peak)
        met.append((s, values, seen))
    sums = acc_ref[rows, :] * jnp.exp2((before - peak) * factor)
    weights = [jnp.exp2((s - jnp.where(seen, peak, -MASKED_SCORE)) * factor) for s, _, seen in met]
    mixed = mix(jnp.concatenate(weights, axis=1), jnp.concatenate([v for _, v, _ in met], axis=0))
    return jnp.broadcast_to(peak, (block, LANES)), sums + mixed


def earlier_kernel(
    heads, block, scale, meta_ref, row_ref, first_ref, q_ref, far_ref, over_ref, near_ref, peak_in, acc_in,
    out_ref, log_ref, peak_ref, acc_ref, cols_ref,
):
    del peak_in, acc_in
    factor = scale * LOG2E
    count = q_ref.shape[0]
    span = count // heads
    begin = first_ref[0]
    base = meta_ref[0]

    def shard(distance, which):
        if distance == 2:
            pieces = [r[c, which] for r in (far_ref, over_ref) for c in range(2)]
        else:
            pieces = [near_ref[0 if distance == 1 else 1, i, which] for i in range(4)]
        return jnp.concatenate(pieces, axis=0)

    def seen_rows(rows_first):
        return rows_first + lax.broadcasted_iota(jnp.int32, (block, 1), 0) < first_ref[1]

    def finish(rows, peak, sums):
        total = sums[:, LANES:]
        out_ref[rows, :] = (sums[:, :LANES] / total).astype(out_ref.dtype)
        cols_ref[rows, :] = peak * scale + jnp.log(total)

    whole = begin <= base - (GROUP - 1) * span

    @pl.when(whole)
    def _():
        parts = [(shard(d, 0), with_ones(shard(d, 1))) for d in (1, 2, 3)]
        for i in range(0, count, block):
            rows = pl.ds(i, block)
            chunks = [(keys, values, seen_rows(i), None) for keys, values in parts]
            finish(rows, *block_sums(rows, block, peak_ref, acc_ref, q_ref, chunks, factor))

    @pl.when(jnp.logical_not(whole))
    def _():
        for distance in (1, 2, 3):

            @pl.when(begin < base - (distance - 1) * span)
            def _():
                keys, values = shard(distance, 0), with_ones(shard(distance, 1))
                at = lax.broadcasted_iota(jnp.int32, (1, span), 1)
                if distance == 2:
                    half = span // 2
                    at = jnp.where(at < half, at + row_ref[0] * half, at - row_ref[0] * half)
                seen_keys = base - distance * span + at >= begin
                for i in range(0, count, block):
                    rows = pl.ds(i, block)
                    chunks = [(keys, values, seen_rows(i), seen_keys)]
                    peak, sums = block_sums(rows, block, peak_ref, acc_ref, q_ref, chunks, factor)
                    peak_ref[rows, :] = peak
                    acc_ref[rows, :] = sums

        for i in range(0, count, block):
            rows = pl.ds(i, block)
            finish(rows, peak_ref[rows, :], acc_ref[rows, :])

    eye = lax.broadcasted_iota(jnp.int32, (LANES, LANES), 0) == lax.broadcasted_iota(jnp.int32, (LANES, LANES), 1)
    for h in range(heads):
        for j in range(span // LANES):
            tall = cols_ref[pl.ds(j * LANES * heads + h, LANES, stride=heads), :]
            log_ref[h : h + 1, j * LANES : (j + 1) * LANES] = jnp.sum(
                jnp.where(eye, tall, 0.0), axis=0, keepdims=True
            )


def place(s, z, c):
    return (s * 2 + z) * 2 + c


def permuted(value, source):
    pairs = []
    for s in range(GROUP):
        for z in range(2):
            for c in range(2):
                at = source(s, z, c)
                if at is not None and at[0] >= 0:
                    pairs.append((place(*at), place(s, z, c)))
    return lax.ppermute(value, ("s", "z", "c"), pairs)


def per_device(queries, keys_values, doc_start):
    span, heads, width = queries.shape
    count = span * heads
    scale = width ** (-0.5)
    tokens = 128
    shard = lax.axis_index("g") * GROUP + lax.axis_index("s")
    meta = (shard * span).astype(jnp.int32).reshape(1)
    flat_q = queries.reshape(count, width)
    starts = doc_start.reshape(span // LANES, LANES)

    row = lax.axis_index("z").astype(jnp.int32).reshape(1)
    state = (
        jax.ShapeDtypeStruct((count, LANES), jnp.float32),
        jax.ShapeDtypeStruct((count, 2 * width), jnp.float32),
    )
    smem = pl.BlockSpec(memory_space=pltpu.SMEM)
    vmem = pl.BlockSpec(memory_space=pltpu.VMEM)
    params = pltpu.CompilerParams(vmem_limit_bytes=32 * 1024 * 1024)

    far = permuted(keys_values, lambda s, z, c: (s - 2, z, c))
    own = lax.all_gather(keys_values, ("z", "c"), axis=0)
    own, far = lax.optimization_barrier((own, far))
    near = permuted(own, lambda s, z, c: (s - 1, z, c) if c == 0 else (s - 3, z, c))
    far = lax.all_gather(far, "c", axis=0)
    over = permuted(far, lambda s, z, c: (s, 1 - z, c) if s >= 2 else None)
    peak, acc, first = pl.pallas_call(
        functools.partial(own_kernel, heads, tokens, scale),
        out_shape=(*state, jax.ShapeDtypeStruct((2,), jnp.int32)),
        in_specs=[smem, vmem, vmem, vmem],
        out_specs=(vmem, vmem, smem),
        scratch_shapes=[pltpu.VMEM((count, LANES), jnp.float32)],
        compiler_params=params,
        cost_estimate=pl.CostEstimate(flops=600_000_000, bytes_accessed=4_000_000, transcendentals=700_000),
    )(meta, starts, flat_q, own)
    near = lax.all_gather(near, "c", axis=0)
    out, log_total, _, _ = pl.pallas_call(
        functools.partial(earlier_kernel, heads, 256, scale),
        out_shape=(
            jax.ShapeDtypeStruct((count, width), jnp.bfloat16),
            jax.ShapeDtypeStruct((heads, span), jnp.float32),
            *state,
        ),
        in_specs=[smem, smem, smem] + [vmem] * 6,
        out_specs=(vmem,) * 4,
        input_output_aliases={7: 2, 8: 3},
        scratch_shapes=[pltpu.VMEM((count, LANES), jnp.float32)],
        compiler_params=params,
        cost_estimate=pl.CostEstimate(flops=4_000_000_000, bytes_accessed=6_000_000, transcendentals=4_000_000),
    )(meta, row, first, flat_q, far, over, near, peak, acc)
    return out.reshape(span, heads, width), log_total


def solution(mesh):
    grid = mesh.devices.reshape(-1, GROUP, 2, 2)
    return jax.shard_map(
        per_device,
        mesh=Mesh(grid, ("g", "s", "z", "c")),
        in_specs=(P(("g", "s"), ("z", "c"), None), P(None, ("g", "s", "z", "c"), None), P(("g", "s"))),
        out_specs=(P(("g", "s"), ("z", "c"), None), P(("z", "c"), ("g", "s"))),
        check_vma=False,
    )
```

time: 35.6 us -> 31.3 us (0.88)
  the two profiles are of different devices: /device:TPU:5 before, /device:TPU:165 now
where the time goes in v3:
time: 31.3 us; the launch traced here: 31 us
  blocking collectives  14.9 us (48%)
  Pallas kernels  8.44 us (27%)
  starting transfers between devices  5.32 us (17%)
  local copies, waits for them, and re-layouts  1.68 us (5%)
  between operations  0.69 us (2%)
    all_gather x1, blocking collectives, per_device(): own = lax.all_gather(keys_values, ('z', 'c'), axis=0)  8.06 us
    pallas_call x1, Pallas kernels, per_device(): pl.pallas_call(functools.partial(earlier_kernel, heads, 256, scale), out_...  6.04 us
    ppermute x3, starting transfers between devices, permuted(): return lax.ppermute(value, ('s', 'z', 'c'), pairs)  5.32 us
    all_gather x1, blocking collectives, per_device(): far = lax.all_gather(far, 'c', axis=0)  4.17 us
    all_gather x1, blocking collectives, per_device(): near = lax.all_gather(near, 'c', axis=0)  2.63 us
    pallas_call x1, Pallas kernels, per_device(): pl.pallas_call(functools.partial(own_kernel, heads, tokens, scale), out_s...  2.4 us
    unnamed x6, local copies, waits for them, and re-layouts  1.68 us
  transfers between devices with their start and end apart: 3, of which 0 were waited for; matrix products, arithmetic and copies ran while one was open for 0% of the time, Pallas kernels for 8%

profile of v3, /device:TPU:165, one launch (start us, length us, event | category | flops | bytes accessed | tf_op | source)
XLA Modules:
  0.0 31.0 jit_solution(12504367792697039744)
XLA Ops:
  0.6 1.3 %collective-permute-start = (bf16[2,192,128]{2,1,0:T(8,128)(2,1)}, bf16[2,192,128]{2,1,0:T(8,128)(2,1)S(1)}, u32[]{:S(2)}, u32[]{:S(2)}) collective-permute-start(bf16[2,192,128]{2,1,0:T(8,128)(2,1)} %param.4), channel_id=1, source_target_pairs={{0,8},{1,9},{2,10},{3,11},{4,12},{5,13},{6,14},{7,15},{16,24},{17,... | collective-permute-start | bytes 294920 | tf_op jit(solution)/shard_map/ppermute | solution.py:167
  1.9 8.1 %all-gather = bf16[8,192,128]{2,1,0:T(8,128)(2,1)S(1)} all-gather(bf16[2,192,128]{2,1,0:T(8,128)(2,1)} %param.4), channel_id=2, replica_groups=mesh['g'=32,'s'=4,'z'=2,'c'=2] {'z','c'}, dimensions={0}, use_global_device_ids=true | all-gather | bytes 491520 | tf_op jit(solution)/shard_map/all_gather | solution.py:190
  10.0 0.0 collective-permute-done
  10.0 0.7 %collective-permute-start.2 = (bf16[4,2,192,128]{3,2,1,0:T(8,128)(2,1)S(1)}, bf16[4,2,192,128]{3,2,1,0:T(8,128)(2,1)S(1)}, u32[]{:S(2)}, u32[]{:S(2)}) collective-permute-start(bf16[4,2,192,128]{3,2,1,0:T(8,128)(2,1)S(1)} %bitcast.9), channel_id=1, source_target_pairs={{0,4},{2,6},{4,8},{6,10},{8,12},{1,13},{10,14},{3,15},{16,20},{18,... | collective-permute-start | bytes 1179656 | tf_op jit(solution)/shard_map/ppermute | solution.py:167
  10.7 4.2 %all-gather.1 = bf16[4,192,128]{2,1,0:T(8,128)(2,1)S(1)} all-gather(bf16[2,192,128]{2,1,0:T(8,128)(2,1)S(1)} %collective-permute-done), channel_id=3, replica_groups=mesh['g'=32,'s'=4,'z'=2,'c'=2] {'c'}, dimensions={0}, use_global_device_ids=true | all-gather | bytes 294912 | tf_op jit(solution)/shard_map/all_gather | solution.py:193
  14.9 3.4 %collective-permute-start.1 = (bf16[2,2,192,128]{3,2,1,0:T(8,128)(2,1)S(1)}, bf16[2,2,192,128]{3,2,1,0:T(8,128)(2,1)S(1)}, u32[]{:S(2)}, u32[]{:S(2)}) collective-permute-start(bf16[2,2,192,128]{3,2,1,0:T(8,128)(2,1)S(1)} %bitcast.11), channel_id=1, source_target_pairs={{10,8},{11,9},{8,10},{9,11},{14,12},{15,13},{12,14},{13,15},{26,24... | collective-permute-start | bytes 589832 | tf_op jit(solution)/shard_map/ppermute | solution.py:167
  18.2 0.0 copy-start
  18.2 1.0 %copy-done = bf16[768,2,128]{2,1,0:T(2,128)(2,1)S(1)} copy-done((bf16[768,2,128]{2,1,0:T(2,128)(2,1)S(1)}, bf16[768,2,128]{2,1,0:T(2,128)(2,1)}, u32[]{:S(2)}) %copy-start) | copy-done | bytes 393240
  19.2 0.0 copy-start.2
  19.2 0.7 %copy-done.2 = s32[768]{0:T(1024)S(1)} copy-done((s32[768]{0:T(1024)S(1)}, s32[768]{0:T(1024)}, u32[]{:S(2)}) %copy-start.2) | copy-done | bytes 3096
  19.9 0.0 copy-start.1
  19.9 2.4 %shard_map.50 = (f32[1536,128]{1,0:T(8,128)S(1)}, f32[1536,256]{1,0:T(8,128)S(1)}, s32[2]{0:T(128)S(1)}) custom-call(s32[1]{0:T(128)} %bitcast.meta_ref, s32[6,128]{1,0:T(8,128)S(1)} %bitcast.15, bf16[1536,128]{1,0:T(8,128)(2,1)S(1)} %bitcast.13, bf16[4,2,192,128]{3,2,1,0:T(8,128)(2,1)S(1)} %bitcast.10), custom_call_target="tpu_custom_call" | custom-call | flops 600000000 | bytes 4000000 | tf_op jit(solution)/shard_map/pallas_call | solution.py:195
  22.3 0.0 collective-permute-done.2
  22.3 2.6 %all-gather.2 = bf16[8,2,192,128]{3,2,1,0:T(8,128)(2,1)S(1)} all-gather(bf16[4,2,192,128]{3,2,1,0:T(8,128)(2,1)S(1)} %collective-permute-done.2), channel_id=4, replica_groups=mesh['g'=32,'s'=4,'z'=2,'c'=2] {'c'}, dimensions={0}, use_global_device_ids=true | all-gather | bytes 1179648 | tf_op jit(solution)/shard_map/all_gather | solution.py:204
  25.0 0.0 collective-permute-done.1.over_ref
  25.0 0.0 copy-done.1
  25.0 6.0 %shard_map.51 = (bf16[1536,128]{1,0:T(8,128)(2,1)}, f32[2,768]{1,0:T(2,128)}, f32[1536,128]{1,0:T(8,128)S(1)}, f32[1536,256]{1,0:T(8,128)S(1)}) custom-call(s32[1]{0:T(128)} %bitcast.meta_ref, s32[1]{0:T(128)} %bitcast.1.row_ref, s32[2]{0:T(128)S(1)} %get-tuple-element.10.first_ref, ...), custom_call_target="tpu_custom_call", output_to_operand_aliasing={{2}: (7, {}), {3}: (8, {})} | custom-call | flops 4000000000 | bytes 6000000 | tf_op jit(solution)/shard_map/pallas_call | solution.py:205
Async XLA Ops:
  0.6 9.4 %collective-permute-start = (bf16[2,192,128]{2,1,0:T(8,128)(2,1)}, bf16[2,192,128]{2,1,0:T(8,128)(2,1)S(1)}, u32[]{:S(2)}, u32[]{:S(2)}) collective-permute-start(bf16[2,192,128]{2,1,0:T(8,128)(2,1)} %param.4), channel_id=1, source_target_pairs={{0,8},{1,9},{2,10},{3,11},{4,12},{5,13},{6,14},{7,15},{16,24},{17,... | collective-permute-start | bytes 294920 | tf_op jit(solution)/shard_map/ppermute | solution.py:167
  10.0 12.3 %collective-permute-start.2 = (bf16[4,2,192,128]{3,2,1,0:T(8,128)(2,1)S(1)}, bf16[4,2,192,128]{3,2,1,0:T(8,128)(2,1)S(1)}, u32[]{:S(2)}, u32[]{:S(2)}) collective-permute-start(bf16[4,2,192,128]{3,2,1,0:T(8,128)(2,1)S(1)} %bitcast.9), channel_id=1, source_target_pairs={{0,4},{2,6},{4,8},{6,10},{8,12},{1,13},{10,14},{3,15},{16,20},{18,... | collective-permute-start | bytes 1179656 | tf_op jit(solution)/shard_map/ppermute | solution.py:167
  14.9 10.1 %collective-permute-start.1 = (bf16[2,2,192,128]{3,2,1,0:T(8,128)(2,1)S(1)}, bf16[2,2,192,128]{3,2,1,0:T(8,128)(2,1)S(1)}, u32[]{:S(2)}, u32[]{:S(2)}) collective-permute-start(bf16[2,2,192,128]{3,2,1,0:T(8,128)(2,1)S(1)} %bitcast.11), channel_id=1, source_target_pairs={{10,8},{11,9},{8,10},{9,11},{14,12},{15,13},{12,14},{13,15},{26,24... | collective-permute-start | bytes 589832 | tf_op jit(solution)/shard_map/ppermute | solution.py:167
  18.2 1.0 %copy-start = (bf16[768,2,128]{2,1,0:T(2,128)(2,1)S(1)}, bf16[768,2,128]{2,1,0:T(2,128)(2,1)}, u32[]{:S(2)}) copy-start(bf16[768,2,128]{2,1,0:T(2,128)(2,1)} %param.3) | copy-start | bytes 1179652
  19.2 0.7 %copy-start.2 = (s32[768]{0:T(1024)S(1)}, s32[768]{0:T(1024)}, u32[]{:S(2)}) copy-start(s32[768]{0:T(1024)} %param.5) | copy-start | bytes 9220
  19.9 5.1 %copy-start.1 = (bf16[768,2,128]{2,1,0:T(2,128)(2,1)S(1)}, bf16[768,2,128]{2,1,0:T(2,128)(2,1)}, u32[]{:S(2)}) copy-start(bf16[768,2,128]{2,1,0:T(2,128)(2,1)} %param.3) | copy-start | bytes 1179652

commit v4 on v3

v4 whole, which is shorter than its diff:
```python
import functools
import math

import jax
import jax.numpy as jnp
from jax import lax
from jax.experimental import pallas as pl
from jax.experimental.pallas import tpu as pltpu
from jax.sharding import Mesh, PartitionSpec as P

GROUP = 4
MASKED_SCORE = -1e30
LOG2E = math.log2(math.e)
LANES = 128


def starts_kernel(heads, meta_ref, starts_ref, cols_ref, first_ref):
    starts = starts_ref[...].astype(jnp.float32)
    begin = jnp.min(starts)
    first_ref[0] = begin.astype(jnp.int32)
    first_ref[1] = jnp.sum(jnp.where(starts == begin, 1.0, 0.0)).astype(jnp.int32) * heads
    starts = starts - meta_ref[0].astype(jnp.float32)
    for j in range(starts.shape[0]):
        tall = jnp.transpose(jnp.broadcast_to(starts[j : j + 1, :], (LANES, LANES)))
        for h in range(heads):
            cols_ref[pl.ds(j * LANES * heads + h, LANES, stride=heads), :] = tall


def scores_of(q, keys):
    return lax.dot_general(q, keys, (((1,), (1,)), ((), ())), preferred_element_type=jnp.float32)


def with_ones(values):
    return jnp.concatenate([values, jnp.ones_like(values)], axis=1)


def mix(weights, values):
    return lax.dot_general(
        weights.astype(jnp.bfloat16), values, (((1,), (0,)), ((), ())), preferred_element_type=jnp.float32
    )


def own_kernel(heads, scale, cols_ref, q_ref, kv_ref, peak_ref, acc_ref):
    factor = scale * LOG2E
    pieces = kv_ref.shape[0]
    keys = jnp.concatenate([kv_ref[i, 0] for i in range(pieces)], axis=0)
    values = with_ones(jnp.concatenate([kv_ref[i, 1] for i in range(pieces)], axis=0))
    block = LANES * heads
    shape = (block, LANES)
    lane = lax.broadcasted_iota(jnp.int32, shape, 1)
    causal = lane <= lax.broadcasted_iota(jnp.int32, shape, 0) // heads
    blocks = q_ref.shape[0] // block

    def scores(i):
        rows = pl.ds(i * block, block)
        s = scores_of(q_ref[rows, :], keys[: (i + 1) * LANES])
        cols = cols_ref[rows, :]
        parts = []
        for j in range(i + 1):
            visible = (lane + j * LANES).astype(jnp.float32) >= cols
            visible = visible & causal if j == i else visible
            parts.append(jnp.where(visible, s[:, j * LANES : (j + 1) * LANES], MASKED_SCORE))
        return jnp.concatenate(parts, axis=1)

    ahead = scores(0)
    for i in range(blocks):
        rows, s = pl.ds(i * block, block), ahead
        if i + 1 < blocks:
            ahead = scores(i + 1)
        peak = jnp.max(s, axis=1, keepdims=True)
        weights = jnp.exp2((s - peak) * factor)
        peak_ref[rows, :] = jnp.broadcast_to(peak, shape)
        acc_ref[rows, :] = mix(weights, values[: (i + 1) * LANES])


def block_sums(rows, block, peak_ref, acc_ref, s, values, seen, factor):
    before = peak_ref[rows, :1]
    reached = jnp.maximum(before, jnp.max(s, axis=1, keepdims=True))
    peak = jnp.where(seen, reached, before)
    weights = jnp.exp2((s - jnp.where(seen, reached, -MASKED_SCORE)) * factor)
    sums = acc_ref[rows, :] * jnp.exp2((before - peak) * factor) + mix(weights, values)
    return jnp.broadcast_to(peak, (block, LANES)), sums


def earlier_kernel(
    heads, block, scale, meta_ref, row_ref, first_ref, q_ref, far_ref, over_ref, near_ref, peak_in, acc_in,
    out_ref, log_ref, peak_ref, acc_ref, cols_ref,
):
    del peak_in, acc_in
    factor = scale * LOG2E
    count = q_ref.shape[0]
    span = count // heads
    begin = first_ref[0]
    base = meta_ref[0]

    def shard(distance, which):
        if distance == 2:
            pieces = [r[c, which] for r in (far_ref, over_ref) for c in range(2)]
        else:
            pieces = [near_ref[0 if distance == 1 else 1, i, which] for i in range(4)]
        return jnp.concatenate(pieces, axis=0)

    def seen_rows(rows_first):
        return rows_first + lax.broadcasted_iota(jnp.int32, (block, 1), 0) < first_ref[1]

    def finish(rows, peak, sums):
        total = sums[:, LANES:]
        out_ref[rows, :] = (sums[:, :LANES] / total).astype(out_ref.dtype)
        cols_ref[rows, :] = peak * scale + jnp.log(total)

    def attend(distances, seen_keys, done):
        keys = jnp.concatenate([shard(d, 0) for d in distances], axis=0)
        values = jnp.concatenate([with_ones(shard(d, 1)) for d in distances], axis=0)

        def scores(i):
            s = scores_of(q_ref[pl.ds(i, block), :], keys)
            return s if seen_keys is None else jnp.where(seen_keys, s, MASKED_SCORE)

        ahead = scores(0)
        for i in range(0, count, block):
            rows, s = pl.ds(i, block), ahead
            if i + block < count:
                ahead = scores(i + block)
            done(rows, *block_sums(rows, block, peak_ref, acc_ref, s, values, seen_rows(i), factor))

    def keep(rows, peak, sums):
        peak_ref[rows, :] = peak
        acc_ref[rows, :] = sums

    three = begin <= base - 3 * span
    two = begin == base - 2 * span
    pl.when(three)(functools.partial(attend, (1, 2, 3), None, finish))
    pl.when(two)(functools.partial(attend, (1, 2), None, finish))

    @pl.when(jnp.logical_not(three | two))
    def _():
        for distance in (1, 2, 3):

            @pl.when(begin < base - (distance - 1) * span)
            def _():
                at = lax.broadcasted_iota(jnp.int32, (1, span), 1)
                if distance == 2:
                    half = span // 2
                    at = jnp.where(at < half, at + row_ref[0] * half, at - row_ref[0] * half)
                attend((distance,), base - distance * span + at >= begin, keep)

        for i in range(0, count, block):
            rows = pl.ds(i, block)
            finish(rows, peak_ref[rows, :], acc_ref[rows, :])

    eye = lax.broadcasted_iota(jnp.int32, (LANES, LANES), 0) == lax.broadcasted_iota(jnp.int32, (LANES, LANES), 1)
    for h in range(heads):
        for j in range(span // LANES):
            tall = cols_ref[pl.ds(j * LANES * heads + h, LANES, stride=heads), :]
            log_ref[h : h + 1, j * LANES : (j + 1) * LANES] = jnp.sum(
                jnp.where(eye, tall, 0.0), axis=0, keepdims=True
            )


def place(s, z, c):
    return (s * 2 + z) * 2 + c


def permuted(value, source):
    pairs = []
    for s in range(GROUP):
        for z in range(2):
            for c in range(2):
                at = source(s, z, c)
                if at is not None and at[0] >= 0:
                    pairs.append((place(*at), place(s, z, c)))
    return lax.ppermute(value, ("s", "z", "c"), pairs)


def per_device(queries, keys_values, doc_start):
    span, heads, width = queries.shape
    count = span * heads
    scale = width ** (-0.5)
    shard = lax.axis_index("g") * GROUP + lax.axis_index("s")
    meta = (shard * span).astype(jnp.int32).reshape(1)
    flat_q = queries.reshape(count, width)
    starts = doc_start.reshape(span // LANES, LANES)

    row = lax.axis_index("z").astype(jnp.int32).reshape(1)
    state = (
        jax.ShapeDtypeStruct((count, LANES), jnp.float32),
        jax.ShapeDtypeStruct((count, 2 * width), jnp.float32),
    )
    smem = pl.BlockSpec(memory_space=pltpu.SMEM)
    vmem = pl.BlockSpec(memory_space=pltpu.VMEM)
    params = pltpu.CompilerParams(vmem_limit_bytes=32 * 1024 * 1024)

    far = permuted(keys_values, lambda s, z, c: (s - 2, z, c))
    own = lax.all_gather(keys_values, ("z", "c"), axis=0)
    own, far = lax.optimization_barrier((own, far))
    near = permuted(own, lambda s, z, c: (s - 1, z, 1) if c == 0 else (s - 3, z, 0))
    far = lax.all_gather(far, "c", axis=0)
    over = permuted(far, lambda s, z, c: (s, 1 - z, c) if s >= 2 else None)
    starts, far = lax.optimization_barrier((starts, far))
    cols, first = pl.pallas_call(
        functools.partial(starts_kernel, heads),
        out_shape=(state[0], jax.ShapeDtypeStruct((2,), jnp.int32)),
        in_specs=[smem, vmem],
        out_specs=(vmem, smem),
        compiler_params=params,
        cost_estimate=pl.CostEstimate(flops=400_000_000, bytes_accessed=1_000_000, transcendentals=0),
    )(meta, starts)
    peak, acc = pl.pallas_call(
        functools.partial(own_kernel, heads, scale),
        out_shape=state,
        in_specs=[vmem, vmem, vmem],
        out_specs=(vmem, vmem),
        compiler_params=params,
        cost_estimate=pl.CostEstimate(flops=600_000_000, bytes_accessed=4_000_000, transcendentals=700_000),
    )(cols, flat_q, own)
    near = lax.all_gather(near, "c", axis=0)
    out, log_total, _, _ = pl.pallas_call(
        functools.partial(earlier_kernel, heads, 384, scale),
        out_shape=(
            jax.ShapeDtypeStruct((count, width), jnp.bfloat16),
            jax.ShapeDtypeStruct((heads, span), jnp.float32),
            *state,
        ),
        in_specs=[smem, smem, smem] + [vmem] * 6,
        out_specs=(vmem,) * 4,
        input_output_aliases={7: 2, 8: 3},
        scratch_shapes=[pltpu.VMEM((count, LANES), jnp.float32)],
        compiler_params=params,
        cost_estimate=pl.CostEstimate(flops=4_000_000_000, bytes_accessed=6_000_000, transcendentals=4_000_000),
    )(meta, row, first, flat_q, far, over, near, peak, acc)
    return out.reshape(span, heads, width), log_total


def solution(mesh):
    grid = mesh.devices.reshape(-1, GROUP, 2, 2)
    return jax.shard_map(
        per_device,
        mesh=Mesh(grid, ("g", "s", "z", "c")),
        in_specs=(P(("g", "s"), ("z", "c"), None), P(None, ("g", "s", "z", "c"), None), P(("g", "s"))),
        out_specs=(P(("g", "s"), ("z", "c"), None), P(("z", "c"), ("g", "s"))),
        check_vma=False,
    )
```

time: 31.3 us -> 30.7 us (0.981)
  the two profiles are of different devices: /device:TPU:165 before, /device:TPU:191 now
where the time goes in v4:
time: 30.7 us; the launch traced here: 30.5 us
  blocking collectives  12.4 us (40%)
  Pallas kernels  9.76 us (32%)
  starting transfers between devices  5.87 us (19%)
  waiting for transfers between devices  1.09 us (4%)
  between operations  0.7 us (2%)
  local copies, waits for them, and re-layouts  0.69 us (2%)
    all_gather x1, blocking collectives, per_device(): own = lax.all_gather(keys_values, ('z', 'c'), axis=0)  8.06 us
    pallas_call x1, Pallas kernels, per_device(): pl.pallas_call(functools.partial(earlier_kernel, heads, 384, scale), out_...  7.36 us
    ppermute x3, starting transfers between devices, permuted(): return lax.ppermute(value, ('s', 'z', 'c'), pairs)  5.87 us
    all_gather x1, blocking collectives, per_device(): near = lax.all_gather(near, 'c', axis=0)  2.36 us
    all_gather x1, blocking collectives, per_device(): far = lax.all_gather(far, 'c', axis=0)  1.95 us
    pallas_call x1, Pallas kernels, per_device(): pl.pallas_call(functools.partial(own_kernel, heads, scale), out_shape=sta...  1.57 us
    ppermute x3, waiting for transfers between devices, permuted(): return lax.ppermute(value, ('s', 'z', 'c'), pairs)  1.09 us
    pallas_call x1, Pallas kernels, per_device(): pl.pallas_call(functools.partial(starts_kernel, heads), out_shape=(state[...  0.83 us
  transfers between devices with their start and end apart: 3, of which 1 were waited for; matrix products, arithmetic and copies ran while one was open for 0% of the time, Pallas kernels for 8%

profile of v4, /device:TPU:191, one launch (start us, length us, event | category | flops | bytes accessed | tf_op | source)
XLA Modules:
  0.0 30.5 jit_solution(5199062097829560058)
XLA Ops:
  0.6 0.0 copy-start
  0.6 1.4 %collective-permute-start = (bf16[2,192,128]{2,1,0:T(8,128)(2,1)}, bf16[2,192,128]{2,1,0:T(8,128)(2,1)S(1)}, u32[]{:S(2)}, u32[]{:S(2)}) collective-permute-start(bf16[2,192,128]{2,1,0:T(8,128)(2,1)} %param.4), channel_id=1, source_target_pairs={{0,8},{1,9},{2,10},{3,11},{4,12},{5,13},{6,14},{7,15},{16,24},{17,... | collective-permute-start | bytes 294920 | tf_op jit(solution)/shard_map/ppermute | solution.py:172
  2.1 8.1 %all-gather = bf16[8,192,128]{2,1,0:T(8,128)(2,1)S(1)} all-gather(bf16[2,192,128]{2,1,0:T(8,128)(2,1)} %param.4), channel_id=2, replica_groups=mesh['g'=32,'s'=4,'z'=2,'c'=2] {'z','c'}, dimensions={0}, use_global_device_ids=true | all-gather | bytes 491520 | tf_op jit(solution)/shard_map/all_gather | solution.py:194
  10.1 0.0 collective-permute-done
  10.1 1.3 %collective-permute-start.2 = (bf16[4,2,192,128]{3,2,1,0:T(8,128)(2,1)S(1)}, bf16[4,2,192,128]{3,2,1,0:T(8,128)(2,1)S(1)}, u32[]{:S(2)}, u32[]{:S(2)}) collective-permute-start(bf16[4,2,192,128]{3,2,1,0:T(8,128)(2,1)S(1)} %bitcast.9), channel_id=1, source_target_pairs={{1,4},{3,6},{5,8},{7,10},{9,12},{0,13},{11,14},{2,15},{17,20},{19,... | collective-permute-start | bytes 1179656 | tf_op jit(solution)/shard_map/ppermute | solution.py:172
  11.4 1.9 %all-gather.1 = bf16[4,192,128]{2,1,0:T(8,128)(2,1)S(1)} all-gather(bf16[2,192,128]{2,1,0:T(8,128)(2,1)S(1)} %collective-permute-done), channel_id=3, replica_groups=mesh['g'=32,'s'=4,'z'=2,'c'=2] {'c'}, dimensions={0}, use_global_device_ids=true | all-gather | bytes 294912 | tf_op jit(solution)/shard_map/all_gather | solution.py:197
  13.4 3.2 %collective-permute-start.1 = (bf16[2,2,192,128]{3,2,1,0:T(8,128)(2,1)S(1)}, bf16[2,2,192,128]{3,2,1,0:T(8,128)(2,1)S(1)}, u32[]{:S(2)}, u32[]{:S(2)}) collective-permute-start(bf16[2,2,192,128]{3,2,1,0:T(8,128)(2,1)S(1)} %bitcast.11), channel_id=1, source_target_pairs={{10,8},{11,9},{8,10},{9,11},{14,12},{15,13},{12,14},{13,15},{26,24... | collective-permute-start | bytes 589832 | tf_op jit(solution)/shard_map/ppermute | solution.py:172
  16.6 0.0 copy-start.1
  16.6 0.7 %copy-done.1 = s32[768]{0:T(1024)S(1)} copy-done((s32[768]{0:T(1024)S(1)}, s32[768]{0:T(1024)}, u32[]{:S(2)}) %copy-start.1) | copy-done | bytes 3096
  17.2 0.8 %shard_map.50 = (f32[1536,128]{1,0:T(8,128)S(1)}, s32[2]{0:T(128)S(1)}) custom-call(s32[1]{0:T(128)} %bitcast.meta_ref, s32[6,128]{1,0:T(8,128)S(1)} %bitcast.15), custom_call_target="tpu_custom_call" | custom-call | flops 400000000 | bytes 1000000 | tf_op jit(solution)/shard_map/pallas_call | solution.py:200
  18.1 0.0 copy-done
  18.1 1.6 %shard_map.51 = (f32[1536,128]{1,0:T(8,128)S(1)}, f32[1536,256]{1,0:T(8,128)S(1)}) custom-call(f32[1536,128]{1,0:T(8,128)S(1)} %get-tuple-element.17.cols_ref, bf16[1536,128]{1,0:T(8,128)(2,1)S(1)} %bitcast.13, bf16[4,2,192,128]{3,2,1,0:T(8,128)(2,1)S(1)} %bitcast.10), custom_call_target="tpu_custom_call" | custom-call | flops 600000000 | bytes 4000000 | tf_op jit(solution)/shard_map/pallas_call | solution.py:208
  19.7 1.1 %collective-permute-done.2 = bf16[4,2,192,128]{3,2,1,0:T(8,128)(2,1)S(1)} collective-permute-done((bf16[4,2,192,128]{3,2,1,0:T(8,128)(2,1)S(1)}, bf16[4,2,192,128]{3,2,1,0:T(8,128)(2,1)S(1)}, u32[]{:S(2)}, u32[]{:S(2)}) %collective-permute-start.2) | collective-permute-done | bytes 393248 | tf_op jit(solution)/shard_map/ppermute | solution.py:172
  20.8 2.4 %all-gather.2 = bf16[8,2,192,128]{3,2,1,0:T(8,128)(2,1)S(1)} all-gather(bf16[4,2,192,128]{3,2,1,0:T(8,128)(2,1)S(1)} %collective-permute-done.2), channel_id=4, replica_groups=mesh['g'=32,'s'=4,'z'=2,'c'=2] {'c'}, dimensions={0}, use_global_device_ids=true | all-gather | bytes 1179648 | tf_op jit(solution)/shard_map/all_gather | solution.py:216
  23.1 0.0 collective-permute-done.1.over_ref
  23.1 7.4 %shard_map.52 = (bf16[1536,128]{1,0:T(8,128)(2,1)}, f32[2,768]{1,0:T(2,128)}, f32[1536,128]{1,0:T(8,128)S(1)}, f32[1536,256]{1,0:T(8,128)S(1)}) custom-call(s32[1]{0:T(128)} %bitcast.meta_ref, s32[1]{0:T(128)} %bitcast.1.row_ref, s32[2]{0:T(128)S(1)} %get-tuple-element.14.first_ref, ...), custom_call_target="tpu_custom_call", output_to_operand_aliasing={{2}: (7, {}), {3}: (8, {})} | custom-call | flops 4000000000 | bytes 6000000 | tf_op jit(solution)/shard_map/pallas_call | solution.py:217
Async XLA Ops:
  0.6 17.5 %copy-start = (bf16[768,2,128]{2,1,0:T(2,128)(2,1)S(1)}, bf16[768,2,128]{2,1,0:T(2,128)(2,1)}, u32[]{:S(2)}) copy-start(bf16[768,2,128]{2,1,0:T(2,128)(2,1)} %param.3) | copy-start | bytes 1179652
  0.6 9.5 %collective-permute-start = (bf16[2,192,128]{2,1,0:T(8,128)(2,1)}, bf16[2,192,128]{2,1,0:T(8,128)(2,1)S(1)}, u32[]{:S(2)}, u32[]{:S(2)}) collective-permute-start(bf16[2,192,128]{2,1,0:T(8,128)(2,1)} %param.4), channel_id=1, source_target_pairs={{0,8},{1,9},{2,10},{3,11},{4,12},{5,13},{6,14},{7,15},{16,24},{17,... | collective-permute-start | bytes 294920 | tf_op jit(solution)/shard_map/ppermute | solution.py:172
  10.1 10.6 %collective-permute-start.2 = (bf16[4,2,192,128]{3,2,1,0:T(8,128)(2,1)S(1)}, bf16[4,2,192,128]{3,2,1,0:T(8,128)(2,1)S(1)}, u32[]{:S(2)}, u32[]{:S(2)}) collective-permute-start(bf16[4,2,192,128]{3,2,1,0:T(8,128)(2,1)S(1)} %bitcast.9), channel_id=1, source_target_pairs={{1,4},{3,6},{5,8},{7,10},{9,12},{0,13},{11,14},{2,15},{17,20},{19,... | collective-permute-start | bytes 1179656 | tf_op jit(solution)/shard_map/ppermute | solution.py:172
  13.4 9.7 %collective-permute-start.1 = (bf16[2,2,192,128]{3,2,1,0:T(8,128)(2,1)S(1)}, bf16[2,2,192,128]{3,2,1,0:T(8,128)(2,1)S(1)}, u32[]{:S(2)}, u32[]{:S(2)}) collective-permute-start(bf16[2,2,192,128]{3,2,1,0:T(8,128)(2,1)S(1)} %bitcast.11), channel_id=1, source_target_pairs={{10,8},{11,9},{8,10},{9,11},{14,12},{15,13},{12,14},{13,15},{26,24... | collective-permute-start | bytes 589832 | tf_op jit(solution)/shard_map/ppermute | solution.py:172
  16.6 0.7 %copy-start.1 = (s32[768]{0:T(1024)S(1)}, s32[768]{0:T(1024)}, u32[]{:S(2)}) copy-start(s32[768]{0:T(1024)} %param.5) | copy-start | bytes 9220

commit v5 on v4

--- a/solution.py
+++ b/solution.py
@@ -14,12 +14,16 @@
 LANES = 128
 
 
-def starts_kernel(heads, meta_ref, starts_ref, cols_ref, first_ref):
+def starts_kernel(heads, starts_ref, cols_ref, first_ref):
+    span = starts_ref.shape[0] * LANES
+    base = (lax.axis_index("g") * GROUP + lax.axis_index("s")) * span
     starts = starts_ref[...].astype(jnp.float32)
     begin = jnp.min(starts)
     first_ref[0] = begin.astype(jnp.int32)
     first_ref[1] = jnp.sum(jnp.where(starts == begin, 1.0, 0.0)).astype(jnp.int32) * heads
-    starts = starts - meta_ref[0].astype(jnp.float32)
+    first_ref[2] = base
+    first_ref[3] = lax.axis_index("z")
+    starts = starts - base.astype(jnp.float32)
     for j in range(starts.shape[0]):
         tall = jnp.transpose(jnp.broadcast_to(starts[j : j + 1, :], (LANES, LANES)))
         for h in range(heads):
@@ -82,8 +86,16 @@
     return jnp.broadcast_to(peak, (block, LANES)), sums
 
 
+def row_blocks(count):
+    parts, blocks, first = (2, 3, 3, 3, 1), [], 0
+    for part in parts:
+        blocks.append((first, count * part // sum(parts)))
+        first += blocks[-1][1]
+    return blocks
+
+
 def earlier_kernel(
-    heads, block, scale, meta_ref, row_ref, first_ref, q_ref, far_ref, over_ref, near_ref, peak_in, acc_in,
+    heads, blocks, scale, first_ref, q_ref, far_ref, over_ref, near_ref, peak_in, acc_in,
     out_ref, log_ref, peak_ref, acc_ref, cols_ref,
 ):
     del peak_in, acc_in
@@ -91,7 +103,7 @@
     count = q_ref.shape[0]
     span = count // heads
     begin = first_ref[0]
-    base = meta_ref[0]
+    base = first_ref[2]
 
     def shard(distance, which):
         if distance == 2:
@@ -100,7 +112,7 @@
             pieces = [near_ref[0 if distance == 1 else 1, i, which] for i in range(4)]
         return jnp.concatenate(pieces, axis=0)
 
-    def seen_rows(rows_first):
+    def seen_rows(rows_first, block):
         return rows_first + lax.broadcasted_iota(jnp.int32, (block, 1), 0) < first_ref[1]
 
     def finish(rows, peak, sums):
@@ -108,43 +120,36 @@
         out_ref[rows, :] = (sums[:, :LANES] / total).astype(out_ref.dtype)
         cols_ref[rows, :] = peak * scale + jnp.log(total)
 
-    def attend(distances, seen_keys, done):
-        keys = jnp.concatenate([shard(d, 0) for d in distances], axis=0)
-        values = jnp.concatenate([with_ones(shard(d, 1)) for d in distances], axis=0)
-
-        def scores(i):
+    def attend(reach):
+        keys = jnp.concatenate([shard(d, 0) for d in range(1, reach + 1)], axis=0)
+        values = jnp.concatenate([with_ones(shard(d, 1)) for d in range(1, reach + 1)], axis=0)
+        at = lax.broadcasted_iota(jnp.int32, (1, span), 1)
+        if reach == 2:
+            half = span // 2
+            at = jnp.where(at < half, at + first_ref[3] * half, at - first_ref[3] * half)
+        seen_keys = base - reach * span + at >= begin
+        clear = (reach - 1) * span
+
+        def scores(i, block):
             s = scores_of(q_ref[pl.ds(i, block), :], keys)
-            return s if seen_keys is None else jnp.where(seen_keys, s, MASKED_SCORE)
-
-        ahead = scores(0)
-        for i in range(0, count, block):
+            last = jnp.where(seen_keys, s[:, clear:], MASKED_SCORE)
+            return jnp.concatenate([s[:, :clear], last], axis=1) if clear else last
+
+        ahead = scores(*blocks[0])
+        for n, (i, block) in enumerate(blocks):
             rows, s = pl.ds(i, block), ahead
-            if i + block < count:
-                ahead = scores(i + block)
-            done(rows, *block_sums(rows, block, peak_ref, acc_ref, s, values, seen_rows(i), factor))
-
-    def keep(rows, peak, sums):
-        peak_ref[rows, :] = peak
-        acc_ref[rows, :] = sums
-
-    three = begin <= base - 3 * span
-    two = begin == base - 2 * span
-    pl.when(three)(functools.partial(attend, (1, 2, 3), None, finish))
-    pl.when(two)(functools.partial(attend, (1, 2), None, finish))
-
-    @pl.when(jnp.logical_not(three | two))
+            if n + 1 < len(blocks):
+                ahead = scores(*blocks[n + 1])
+            finish(rows, *block_sums(rows, block, peak_ref, acc_ref, s, values, seen_rows(i, block), factor))
+
+    for reach in (1, 2, 3):
+        enters = begin < base - (reach - 1) * span
+        enters = enters & (begin >= base - reach * span) if reach < 3 else enters
+        pl.when(enters)(functools.partial(attend, reach))
+
+    @pl.when(begin >= base)
     def _():
-        for distance in (1, 2, 3):
-
-            @pl.when(begin < base - (distance - 1) * span)
-            def _():
-                at = lax.broadcasted_iota(jnp.int32, (1, span), 1)
-                if distance == 2:
-                    half = span // 2
-                    at = jnp.where(at < half, at + row_ref[0] * half, at - row_ref[0] * half)
-                attend((distance,), base - distance * span + at >= begin, keep)
-
-        for i in range(0, count, block):
+        for i, block in blocks:
             rows = pl.ds(i, block)
             finish(rows, peak_ref[rows, :], acc_ref[rows, :])
 
@@ -176,12 +181,9 @@
     span, heads, width = queries.shape
     count = span * heads
     scale = width ** (-0.5)
-    shard = lax.axis_index("g") * GROUP + lax.axis_index("s")
-    meta = (shard * span).astype(jnp.int32).reshape(1)
     flat_q = queries.reshape(count, width)
     starts = doc_start.reshape(span // LANES, LANES)
 
-    row = lax.axis_index("z").astype(jnp.int32).reshape(1)
     state = (
         jax.ShapeDtypeStruct((count, LANES), jnp.float32),
         jax.ShapeDtypeStruct((count, 2 * width), jnp.float32),
@@ -199,12 +201,12 @@
     starts, far = lax.optimization_barrier((starts, far))
     cols, first = pl.pallas_call(
         functools.partial(starts_kernel, heads),
-        out_shape=(state[0], jax.ShapeDtypeStruct((2,), jnp.int32)),
-        in_specs=[smem, vmem],
+        out_shape=(state[0], jax.ShapeDtypeStruct((4,), jnp.int32)),
+        in_specs=[vmem],
         out_specs=(vmem, smem),
         compiler_params=params,
         cost_estimate=pl.CostEstimate(flops=400_000_000, bytes_accessed=1_000_000, transcendentals=0),
-    )(meta, starts)
+    )(starts)
     peak, acc = pl.pallas_call(
         functools.partial(own_kernel, heads, scale),
         out_shape=state,
@@ -215,19 +217,19 @@
     )(cols, flat_q, own)
     near = lax.all_gather(near, "c", axis=0)
     out, log_total, _, _ = pl.pallas_call(
-        functools.partial(earlier_kernel, heads, 384, scale),
+        functools.partial(earlier_kernel, heads, row_blocks(count), scale),
         out_shape=(
             jax.ShapeDtypeStruct((count, width), jnp.bfloat16),
             jax.ShapeDtypeStruct((heads, span), jnp.float32),
             *state,
         ),
-        in_specs=[smem, smem, smem] + [vmem] * 6,
+        in_specs=[smem] + [vmem] * 6,
         out_specs=(vmem,) * 4,
-        input_output_aliases={7: 2, 8: 3},
+        input_output_aliases={5: 2, 6: 3},
         scratch_shapes=[pltpu.VMEM((count, LANES), jnp.float32)],
         compiler_params=params,
         cost_estimate=pl.CostEstimate(flops=4_000_000_000, bytes_accessed=6_000_000, transcendentals=4_000_000),
-    )(meta, row, first, flat_q, far, over, near, peak, acc)
+    )(first, flat_q, far, over, near, peak, acc)
     return out.reshape(span, heads, width), log_total
 
 

time: 30.7 us -> 29.9 us (0.974)
  the two profiles are of different devices: /device:TPU:191 before, /device:TPU:7 now
where the time goes in v5:
time: 29.9 us; the launch traced here: 29.7 us
  blocking collectives  12.4 us (41%)
  Pallas kernels  8.46 us (28%)
  starting transfers between devices  5.87 us (20%)
  waiting for transfers between devices  1.64 us (5%)
  between operations  0.7 us (2%)
  local copies, waits for them, and re-layouts  0.69 us (2%)
    all_gather x1, blocking collectives, per_device(): own = lax.all_gather(keys_values, ('z', 'c'), axis=0)  8.06 us
    pallas_call x1, Pallas kernels, per_device(): pl.pallas_call(functools.partial(earlier_kernel, heads, row_blocks(count)...  6.06 us
    ppermute x3, starting transfers between devices, permuted(): return lax.ppermute(value, ('s', 'z', 'c'), pairs)  5.87 us
    all_gather x1, blocking collectives, per_device(): near = lax.all_gather(near, 'c', axis=0)  2.36 us
    all_gather x1, blocking collectives, per_device(): far = lax.all_gather(far, 'c', axis=0)  1.95 us
    ppermute x3, waiting for transfers between devices, permuted(): return lax.ppermute(value, ('s', 'z', 'c'), pairs)  1.64 us
    pallas_call x1, Pallas kernels, per_device(): pl.pallas_call(functools.partial(own_kernel, heads, scale), out_shape=sta...  1.57 us
    pallas_call x1, Pallas kernels, per_device(): pl.pallas_call(functools.partial(starts_kernel, heads), out_shape=(state[...  0.83 us
  transfers between devices with their start and end apart: 3, of which 1 were waited for; matrix products, arithmetic and copies ran while one was open for 0% of the time, Pallas kernels for 8%

profile of v5, /device:TPU:7, one launch (start us, length us, event | category | flops | bytes accessed | tf_op | source)
XLA Modules:
  0.0 29.7 jit_solution(7302309413839426674)
XLA Ops:
  0.6 0.0 copy-start
  0.6 1.4 %collective-permute-start = (bf16[2,192,128]{2,1,0:T(8,128)(2,1)}, bf16[2,192,128]{2,1,0:T(8,128)(2,1)S(1)}, u32[]{:S(2)}, u32[]{:S(2)}) collective-permute-start(bf16[2,192,128]{2,1,0:T(8,128)(2,1)} %param.4), channel_id=1, source_target_pairs={{0,8},{1,9},{2,10},{3,11},{4,12},{5,13},{6,14},{7,15},{16,24},{17,... | collective-permute-start | bytes 294920 | tf_op jit(solution)/shard_map/ppermute | solution.py:177
  2.1 8.1 %all-gather = bf16[8,192,128]{2,1,0:T(8,128)(2,1)S(1)} all-gather(bf16[2,192,128]{2,1,0:T(8,128)(2,1)} %param.4), channel_id=2, replica_groups=mesh['g'=32,'s'=4,'z'=2,'c'=2] {'z','c'}, dimensions={0}, use_global_device_ids=true | all-gather | bytes 491520 | tf_op jit(solution)/shard_map/all_gather | solution.py:196
  10.1 0.0 collective-permute-done
  10.1 1.3 %collective-permute-start.2 = (bf16[4,2,192,128]{3,2,1,0:T(8,128)(2,1)S(1)}, bf16[4,2,192,128]{3,2,1,0:T(8,128)(2,1)S(1)}, u32[]{:S(2)}, u32[]{:S(2)}) collective-permute-start(bf16[4,2,192,128]{3,2,1,0:T(8,128)(2,1)S(1)} %bitcast.7), channel_id=1, source_target_pairs={{1,4},{3,6},{5,8},{7,10},{9,12},{0,13},{11,14},{2,15},{17,20},{19,... | collective-permute-start | bytes 1179656 | tf_op jit(solution)/shard_map/ppermute | solution.py:177
  11.4 1.9 %all-gather.1 = bf16[4,192,128]{2,1,0:T(8,128)(2,1)S(1)} all-gather(bf16[2,192,128]{2,1,0:T(8,128)(2,1)S(1)} %collective-permute-done), channel_id=3, replica_groups=mesh['g'=32,'s'=4,'z'=2,'c'=2] {'c'}, dimensions={0}, use_global_device_ids=true | all-gather | bytes 294912 | tf_op jit(solution)/shard_map/all_gather | solution.py:199
  13.4 3.2 %collective-permute-start.1 = (bf16[2,2,192,128]{3,2,1,0:T(8,128)(2,1)S(1)}, bf16[2,2,192,128]{3,2,1,0:T(8,128)(2,1)S(1)}, u32[]{:S(2)}, u32[]{:S(2)}) collective-permute-start(bf16[2,2,192,128]{3,2,1,0:T(8,128)(2,1)S(1)} %bitcast.9), channel_id=1, source_target_pairs={{10,8},{11,9},{8,10},{9,11},{14,12},{15,13},{12,14},{13,15},{26,24... | collective-permute-start | bytes 589832 | tf_op jit(solution)/shard_map/ppermute | solution.py:177
  16.5 0.0 copy-start.1
  16.6 0.7 %copy-done.1 = s32[768]{0:T(1024)S(1)} copy-done((s32[768]{0:T(1024)S(1)}, s32[768]{0:T(1024)}, u32[]{:S(2)}) %copy-start.1) | copy-done | bytes 3096
  17.2 0.8 %shard_map.50 = (f32[1536,128]{1,0:T(8,128)S(1)}, s32[4]{0:T(128)S(1)}) custom-call(s32[6,128]{1,0:T(8,128)S(1)} %bitcast.13), custom_call_target="tpu_custom_call" | custom-call | flops 400000000 | bytes 1000000 | tf_op jit(solution)/shard_map/pallas_call | solution.py:202
  18.1 0.0 copy-done
  18.1 1.6 %shard_map.51 = (f32[1536,128]{1,0:T(8,128)S(1)}, f32[1536,256]{1,0:T(8,128)S(1)}) custom-call(f32[1536,128]{1,0:T(8,128)S(1)} %get-tuple-element.17.cols_ref, bf16[1536,128]{1,0:T(8,128)(2,1)S(1)} %bitcast.11, bf16[4,2,192,128]{3,2,1,0:T(8,128)(2,1)S(1)} %bitcast.8), custom_call_target="tpu_custom_call" | custom-call | flops 600000000 | bytes 4000000 | tf_op jit(solution)/shard_map/pallas_call | solution.py:210
  19.7 1.6 %collective-permute-done.2 = bf16[4,2,192,128]{3,2,1,0:T(8,128)(2,1)S(1)} collective-permute-done((bf16[4,2,192,128]{3,2,1,0:T(8,128)(2,1)S(1)}, bf16[4,2,192,128]{3,2,1,0:T(8,128)(2,1)S(1)}, u32[]{:S(2)}, u32[]{:S(2)}) %collective-permute-start.2) | collective-permute-done | bytes 393248 | tf_op jit(solution)/shard_map/ppermute | solution.py:177
  21.3 2.4 %all-gather.2 = bf16[8,2,192,128]{3,2,1,0:T(8,128)(2,1)S(1)} all-gather(bf16[4,2,192,128]{3,2,1,0:T(8,128)(2,1)S(1)} %collective-permute-done.2), channel_id=4, replica_groups=mesh['g'=32,'s'=4,'z'=2,'c'=2] {'c'}, dimensions={0}, use_global_device_ids=true | all-gather | bytes 1179648 | tf_op jit(solution)/shard_map/all_gather | solution.py:218
  23.7 0.0 collective-permute-done.1.over_ref
  23.7 6.1 %shard_map.52 = (bf16[1536,128]{1,0:T(8,128)(2,1)}, f32[2,768]{1,0:T(2,128)}, f32[1536,128]{1,0:T(8,128)S(1)}, f32[1536,256]{1,0:T(8,128)S(1)}) custom-call(s32[4]{0:T(128)S(1)} %get-tuple-element.14.first_ref, bf16[1536,128]{1,0:T(8,128)(2,1)S(1)} %bitcast.12, bf16[2,2,192,128]{3,2,1,0:T(8,128)(2,1)S(1)} %bitcast.10, ...), custom_call_target="tpu_custom_call", output_to_operand_aliasing={{2}: (5, {}), {3}: (6, {})} | custom-call | flops 4000000000 | bytes 6000000 | tf_op jit(solution)/shard_map/pallas_call | solution.py:219
Async XLA Ops:
  0.6 17.4 %copy-start = (bf16[768,2,128]{2,1,0:T(2,128)(2,1)S(1)}, bf16[768,2,128]{2,1,0:T(2,128)(2,1)}, u32[]{:S(2)}) copy-start(bf16[768,2,128]{2,1,0:T(2,128)(2,1)} %param.3) | copy-start | bytes 1179652
  0.6 9.5 %collective-permute-start = (bf16[2,192,128]{2,1,0:T(8,128)(2,1)}, bf16[2,192,128]{2,1,0:T(8,128)(2,1)S(1)}, u32[]{:S(2)}, u32[]{:S(2)}) collective-permute-start(bf16[2,192,128]{2,1,0:T(8,128)(2,1)} %param.4), channel_id=1, source_target_pairs={{0,8},{1,9},{2,10},{3,11},{4,12},{5,13},{6,14},{7,15},{16,24},{17,... | collective-permute-start | bytes 294920 | tf_op jit(solution)/shard_map/ppermute | solution.py:177
  10.1 11.2 %collective-permute-start.2 = (bf16[4,2,192,128]{3,2,1,0:T(8,128)(2,1)S(1)}, bf16[4,2,192,128]{3,2,1,0:T(8,128)(2,1)S(1)}, u32[]{:S(2)}, u32[]{:S(2)}) collective-permute-start(bf16[4,2,192,128]{3,2,1,0:T(8,128)(2,1)S(1)} %bitcast.7), channel_id=1, source_target_pairs={{1,4},{3,6},{5,8},{7,10},{9,12},{0,13},{11,14},{2,15},{17,20},{19,... | collective-permute-start | bytes 1179656 | tf_op jit(solution)/shard_map/ppermute | solution.py:177
  13.4 10.3 %collective-permute-start.1 = (bf16[2,2,192,128]{3,2,1,0:T(8,128)(2,1)S(1)}, bf16[2,2,192,128]{3,2,1,0:T(8,128)(2,1)S(1)}, u32[]{:S(2)}, u32[]{:S(2)}) collective-permute-start(bf16[2,2,192,128]{3,2,1,0:T(8,128)(2,1)S(1)} %bitcast.9), channel_id=1, source_target_pairs={{10,8},{11,9},{8,10},{9,11},{14,12},{15,13},{12,14},{13,15},{26,24... | collective-permute-start | bytes 589832 | tf_op jit(solution)/shard_map/ppermute | solution.py:177
  16.5 0.7 %copy-start.1 = (s32[768]{0:T(1024)S(1)}, s32[768]{0:T(1024)}, u32[]{:S(2)}) copy-start(s32[768]{0:T(1024)} %param.5) | copy-start | bytes 9220

commit v6 on v5

--- a/solution.py
+++ b/solution.py
@@ -18,9 +18,8 @@
     span = starts_ref.shape[0] * LANES
     base = (lax.axis_index("g") * GROUP + lax.axis_index("s")) * span
     starts = starts_ref[...].astype(jnp.float32)
-    begin = jnp.min(starts)
-    first_ref[0] = begin.astype(jnp.int32)
-    first_ref[1] = jnp.sum(jnp.where(starts == begin, 1.0, 0.0)).astype(jnp.int32) * heads
+    first_ref[0] = starts_ref[0, 0]
+    first_ref[1] = jnp.sum(jnp.where(starts == starts[:1, :1], 1.0, 0.0)).astype(jnp.int32) * heads
     first_ref[2] = base
     first_ref[3] = lax.axis_index("z")
     starts = starts - base.astype(jnp.float32)
@@ -66,11 +65,11 @@
             parts.append(jnp.where(visible, s[:, j * LANES : (j + 1) * LANES], MASKED_SCORE))
         return jnp.concatenate(parts, axis=1)
 
-    ahead = scores(0)
-    for i in range(blocks):
+    ahead = scores(blocks - 1)
+    for i in reversed(range(blocks)):
         rows, s = pl.ds(i * block, block), ahead
-        if i + 1 < blocks:
-            ahead = scores(i + 1)
+        if i:
+            ahead = scores(i - 1)
         peak = jnp.max(s, axis=1, keepdims=True)
         weights = jnp.exp2((s - peak) * factor)
         peak_ref[rows, :] = jnp.broadcast_to(peak, shape)
@@ -195,7 +194,7 @@
     far = permuted(keys_values, lambda s, z, c: (s - 2, z, c))
     own = lax.all_gather(keys_values, ("z", "c"), axis=0)
     own, far = lax.optimization_barrier((own, far))
-    near = permuted(own, lambda s, z, c: (s - 1, z, 1) if c == 0 else (s - 3, z, 0))
+    near = permuted(own, lambda s, z, c: (s - 1, z, c) if c == 0 else (s - 3, z, c))
     far = lax.all_gather(far, "c", axis=0)
     over = permuted(far, lambda s, z, c: (s, 1 - z, c) if s >= 2 else None)
     starts, far = lax.optimization_barrier((starts, far))

time: 29.9 us -> 29.4 us (0.983)
  Pallas kernels: 8.46 us -> 7.91 us
  transfers between devices with their start and end apart: 3 -> 3, of which waited for: 1 -> 1; matrix products, arithmetic and copies ran while one was open for 0% -> 0% of each run, Pallas kernels for 8% -> 7%
where the time goes in v6:
time: 29.4 us; the launch traced here: 29.2 us
  blocking collectives  12.4 us (42%)
  Pallas kernels  7.91 us (27%)
  starting transfers between devices  5.87 us (20%)
  waiting for transfers between devices  1.68 us (6%)
  local copies, waits for them, and re-layouts  0.69 us (2%)
  between operations  0.69 us (2%)
    all_gather x1, blocking collectives, per_device(): own = lax.all_gather(keys_values, ('z', 'c'), axis=0)  8.06 us
    pallas_call x1, Pallas kernels, per_device(): pl.pallas_call(functools.partial(earlier_kernel, heads, row_blocks(count)...  5.89 us
    ppermute x3, starting transfers between devices, permuted(): return lax.ppermute(value, ('s', 'z', 'c'), pairs)  5.87 us
    all_gather x1, blocking collectives, per_device(): near = lax.all_gather(near, 'c', axis=0)  2.36 us
    all_gather x1, blocking collectives, per_device(): far = lax.all_gather(far, 'c', axis=0)  1.95 us
    ppermute x3, waiting for transfers between devices, permuted(): return lax.ppermute(value, ('s', 'z', 'c'), pairs)  1.68 us
    pallas_call x1, Pallas kernels, per_device(): pl.pallas_call(functools.partial(own_kernel, heads, scale), out_shape=sta...  1.27 us
    pallas_call x1, Pallas kernels, per_device(): pl.pallas_call(functools.partial(starts_kernel, heads), out_shape=(state[...  0.75 us
  transfers between devices with their start and end apart: 3, of which 1 were waited for; matrix products, arithmetic and copies ran while one was open for 0% of the time, Pallas kernels for 7%

profile of v6, /device:TPU:7, one launch (start us, length us, event | category | flops | bytes accessed | tf_op | source)
XLA Modules:
  0.0 29.2 jit_solution(15996878397935191901)
XLA Ops:
  0.6 0.0 copy-start
  0.6 1.4 %collective-permute-start = (bf16[2,192,128]{2,1,0:T(8,128)(2,1)}, bf16[2,192,128]{2,1,0:T(8,128)(2,1)S(1)}, u32[]{:S(2)}, u32[]{:S(2)}) collective-permute-start(bf16[2,192,128]{2,1,0:T(8,128)(2,1)} %param.4), channel_id=1, source_target_pairs={{0,8},{1,9},{2,10},{3,11},{4,12},{5,13},{6,14},{7,15},{16,24},{17,... | collective-permute-start | bytes 294920 | tf_op jit(solution)/shard_map/ppermute | solution.py:176
  2.1 8.1 %all-gather = bf16[8,192,128]{2,1,0:T(8,128)(2,1)S(1)} all-gather(bf16[2,192,128]{2,1,0:T(8,128)(2,1)} %param.4), channel_id=2, replica_groups=mesh['g'=32,'s'=4,'z'=2,'c'=2] {'z','c'}, dimensions={0}, use_global_device_ids=true | all-gather | bytes 491520 | tf_op jit(solution)/shard_map/all_gather | solution.py:195
  10.1 0.0 collective-permute-done
  10.1 1.3 %collective-permute-start.2 = (bf16[4,2,192,128]{3,2,1,0:T(8,128)(2,1)S(1)}, bf16[4,2,192,128]{3,2,1,0:T(8,128)(2,1)S(1)}, u32[]{:S(2)}, u32[]{:S(2)}) collective-permute-start(bf16[4,2,192,128]{3,2,1,0:T(8,128)(2,1)S(1)} %bitcast.7), channel_id=1, source_target_pairs={{0,4},{2,6},{4,8},{6,10},{8,12},{1,13},{10,14},{3,15},{16,20},{18,... | collective-permute-start | bytes 1179656 | tf_op jit(solution)/shard_map/ppermute | solution.py:176
  11.4 1.9 %all-gather.1 = bf16[4,192,128]{2,1,0:T(8,128)(2,1)S(1)} all-gather(bf16[2,192,128]{2,1,0:T(8,128)(2,1)S(1)} %collective-permute-done), channel_id=3, replica_groups=mesh['g'=32,'s'=4,'z'=2,'c'=2] {'c'}, dimensions={0}, use_global_device_ids=true | all-gather | bytes 294912 | tf_op jit(solution)/shard_map/all_gather | solution.py:198
  13.4 3.2 %collective-permute-start.1 = (bf16[2,2,192,128]{3,2,1,0:T(8,128)(2,1)S(1)}, bf16[2,2,192,128]{3,2,1,0:T(8,128)(2,1)S(1)}, u32[]{:S(2)}, u32[]{:S(2)}) collective-permute-start(bf16[2,2,192,128]{3,2,1,0:T(8,128)(2,1)S(1)} %bitcast.9), channel_id=1, source_target_pairs={{10,8},{11,9},{8,10},{9,11},{14,12},{15,13},{12,14},{13,15},{26,24... | collective-permute-start | bytes 589832 | tf_op jit(solution)/shard_map/ppermute | solution.py:176
  16.5 0.0 copy-start.1
  16.6 0.7 %copy-done.1 = s32[768]{0:T(1024)S(1)} copy-done((s32[768]{0:T(1024)S(1)}, s32[768]{0:T(1024)}, u32[]{:S(2)}) %copy-start.1) | copy-done | bytes 3096
  17.2 0.7 %shard_map.50 = (f32[1536,128]{1,0:T(8,128)S(1)}, s32[4]{0:T(128)S(1)}) custom-call(s32[6,128]{1,0:T(8,128)S(1)} %bitcast.13), custom_call_target="tpu_custom_call" | custom-call | flops 400000000 | bytes 1000000 | tf_op jit(solution)/shard_map/pallas_call | solution.py:201
  18.0 0.0 copy-done
  18.0 1.3 %shard_map.51 = (f32[1536,128]{1,0:T(8,128)S(1)}, f32[1536,256]{1,0:T(8,128)S(1)}) custom-call(f32[1536,128]{1,0:T(8,128)S(1)} %get-tuple-element.17.cols_ref, bf16[1536,128]{1,0:T(8,128)(2,1)S(1)} %bitcast.11, bf16[4,2,192,128]{3,2,1,0:T(8,128)(2,1)S(1)} %bitcast.8), custom_call_target="tpu_custom_call" | custom-call | flops 600000000 | bytes 4000000 | tf_op jit(solution)/shard_map/pallas_call | solution.py:209
  19.3 1.7 %collective-permute-done.2 = bf16[4,2,192,128]{3,2,1,0:T(8,128)(2,1)S(1)} collective-permute-done((bf16[4,2,192,128]{3,2,1,0:T(8,128)(2,1)S(1)}, bf16[4,2,192,128]{3,2,1,0:T(8,128)(2,1)S(1)}, u32[]{:S(2)}, u32[]{:S(2)}) %collective-permute-start.2) | collective-permute-done | bytes 393248 | tf_op jit(solution)/shard_map/ppermute | solution.py:176
  21.0 2.4 %all-gather.2 = bf16[8,2,192,128]{3,2,1,0:T(8,128)(2,1)S(1)} all-gather(bf16[4,2,192,128]{3,2,1,0:T(8,128)(2,1)S(1)} %collective-permute-done.2), channel_id=4, replica_groups=mesh['g'=32,'s'=4,'z'=2,'c'=2] {'c'}, dimensions={0}, use_global_device_ids=true | all-gather | bytes 1179648 | tf_op jit(solution)/shard_map/all_gather | solution.py:217
  23.3 0.0 collective-permute-done.1.over_ref
  23.3 5.9 %shard_map.52 = (bf16[1536,128]{1,0:T(8,128)(2,1)}, f32[2,768]{1,0:T(2,128)}, f32[1536,128]{1,0:T(8,128)S(1)}, f32[1536,256]{1,0:T(8,128)S(1)}) custom-call(s32[4]{0:T(128)S(1)} %get-tuple-element.14.first_ref, bf16[1536,128]{1,0:T(8,128)(2,1)S(1)} %bitcast.12, bf16[2,2,192,128]{3,2,1,0:T(8,128)(2,1)S(1)} %bitcast.10, ...), custom_call_target="tpu_custom_call", output_to_operand_aliasing={{2}: (5, {}), {3}: (6, {})} | custom-call | flops 4000000000 | bytes 6000000 | tf_op jit(solution)/shard_map/pallas_call | solution.py:218
Async XLA Ops:
  0.6 17.4 %copy-start = (bf16[768,2,128]{2,1,0:T(2,128)(2,1)S(1)}, bf16[768,2,128]{2,1,0:T(2,128)(2,1)}, u32[]{:S(2)}) copy-start(bf16[768,2,128]{2,1,0:T(2,128)(2,1)} %param.3) | copy-start | bytes 1179652
  0.6 9.5 %collective-permute-start = (bf16[2,192,128]{2,1,0:T(8,128)(2,1)}, bf16[2,192,128]{2,1,0:T(8,128)(2,1)S(1)}, u32[]{:S(2)}, u32[]{:S(2)}) collective-permute-start(bf16[2,192,128]{2,1,0:T(8,128)(2,1)} %param.4), channel_id=1, source_target_pairs={{0,8},{1,9},{2,10},{3,11},{4,12},{5,13},{6,14},{7,15},{16,24},{17,... | collective-permute-start | bytes 294920 | tf_op jit(solution)/shard_map/ppermute | solution.py:176
  10.1 10.8 %collective-permute-start.2 = (bf16[4,2,192,128]{3,2,1,0:T(8,128)(2,1)S(1)}, bf16[4,2,192,128]{3,2,1,0:T(8,128)(2,1)S(1)}, u32[]{:S(2)}, u32[]{:S(2)}) collective-permute-start(bf16[4,2,192,128]{3,2,1,0:T(8,128)(2,1)S(1)} %bitcast.7), channel_id=1, source_target_pairs={{0,4},{2,6},{4,8},{6,10},{8,12},{1,13},{10,14},{3,15},{16,20},{18,... | collective-permute-start | bytes 1179656 | tf_op jit(solution)/shard_map/ppermute | solution.py:176
  13.4 9.9 %collective-permute-start.1 = (bf16[2,2,192,128]{3,2,1,0:T(8,128)(2,1)S(1)}, bf16[2,2,192,128]{3,2,1,0:T(8,128)(2,1)S(1)}, u32[]{:S(2)}, u32[]{:S(2)}) collective-permute-start(bf16[2,2,192,128]{3,2,1,0:T(8,128)(2,1)S(1)} %bitcast.9), channel_id=1, source_target_pairs={{10,8},{11,9},{8,10},{9,11},{14,12},{15,13},{12,14},{13,15},{26,24... | collective-permute-start | bytes 589832 | tf_op jit(solution)/shard_map/ppermute | solution.py:176
  16.5 0.7 %copy-start.1 = (s32[768]{0:T(1024)S(1)}, s32[768]{0:T(1024)}, u32[]{:S(2)}) copy-start(s32[768]{0:T(1024)} %param.5) | copy-start | bytes 9220

commit v7 on v6

--- a/solution.py
+++ b/solution.py
@@ -94,10 +94,9 @@
 
 
 def earlier_kernel(
-    heads, blocks, scale, first_ref, q_ref, far_ref, over_ref, near_ref, peak_in, acc_in,
-    out_ref, log_ref, peak_ref, acc_ref, cols_ref,
+    heads, blocks, scale, first_ref, q_ref, far_ref, over_ref, near_ref, peak_ref, acc_ref,
+    out_ref, log_ref, cols_ref,
 ):
-    del peak_in, acc_in
     factor = scale * LOG2E
     count = q_ref.shape[0]
     span = count // heads
@@ -215,16 +214,14 @@
         cost_estimate=pl.CostEstimate(flops=600_000_000, bytes_accessed=4_000_000, transcendentals=700_000),
     )(cols, flat_q, own)
     near = lax.all_gather(near, "c", axis=0)
-    out, log_total, _, _ = pl.pallas_call(
+    out, log_total = pl.pallas_call(
         functools.partial(earlier_kernel, heads, row_blocks(count), scale),
         out_shape=(
             jax.ShapeDtypeStruct((count, width), jnp.bfloat16),
             jax.ShapeDtypeStruct((heads, span), jnp.float32),
-            *state,
         ),
         in_specs=[smem] + [vmem] * 6,
-        out_specs=(vmem,) * 4,
-        input_output_aliases={5: 2, 6: 3},
+        out_specs=(vmem,) * 2,
         scratch_shapes=[pltpu.VMEM((count, LANES), jnp.float32)],
         compiler_params=params,
         cost_estimate=pl.CostEstimate(flops=4_000_000_000, bytes_accessed=6_000_000, transcendentals=4_000_000),

time: 29.4 us -> 29.4 us (level)
  no operation moved by 1% of the time
where the time goes in v7:
time: 29.4 us; the launch traced here: 29.2 us
  blocking collectives  12.4 us (42%)
  Pallas kernels  7.91 us (27%)
  starting transfers between devices  5.87 us (20%)
  waiting for transfers between devices  1.68 us (6%)
  local copies, waits for them, and re-layouts  0.69 us (2%)
  between operations  0.69 us (2%)
    all_gather x1, blocking collectives, per_device(): own = lax.all_gather(keys_values, ('z', 'c'), axis=0)  8.06 us
    pallas_call x1, Pallas kernels, per_device(): pl.pallas_call(functools.partial(earlier_kernel, heads, row_blocks(count)...  5.89 us
    ppermute x3, starting transfers between devices, permuted(): return lax.ppermute(value, ('s', 'z', 'c'), pairs)  5.87 us
    all_gather x1, blocking collectives, per_device(): near = lax.all_gather(near, 'c', axis=0)  2.36 us
    all_gather x1, blocking collectives, per_device(): far = lax.all_gather(far, 'c', axis=0)  1.95 us
    ppermute x3, waiting for transfers between devices, permuted(): return lax.ppermute(value, ('s', 'z', 'c'), pairs)  1.68 us
    pallas_call x1, Pallas kernels, per_device(): pl.pallas_call(functools.partial(own_kernel, heads, scale), out_shape=sta...  1.27 us
    pallas_call x1, Pallas kernels, per_device(): pl.pallas_call(functools.partial(starts_kernel, heads), out_shape=(state[...  0.75 us
  transfers between devices with their start and end apart: 3, of which 1 were waited for; matrix products, arithmetic and copies ran while one was open for 0% of the time, Pallas kernels for 7%

profile of v7, /device:TPU:7, one launch (start us, length us, event | category | flops | bytes accessed | tf_op | source)
XLA Modules:
  0.0 29.2 jit_solution(5002163582827851723)
XLA Ops:
  0.6 0.0 copy-start
  0.6 1.4 %collective-permute-start = (bf16[2,192,128]{2,1,0:T(8,128)(2,1)}, bf16[2,192,128]{2,1,0:T(8,128)(2,1)S(1)}, u32[]{:S(2)}, u32[]{:S(2)}) collective-permute-start(bf16[2,192,128]{2,1,0:T(8,128)(2,1)} %param.4), channel_id=1, source_target_pairs={{0,8},{1,9},{2,10},{3,11},{4,12},{5,13},{6,14},{7,15},{16,24},{17,... | collective-permute-start | bytes 294920 | tf_op jit(solution)/shard_map/ppermute | solution.py:175
  2.1 8.1 %all-gather = bf16[8,192,128]{2,1,0:T(8,128)(2,1)S(1)} all-gather(bf16[2,192,128]{2,1,0:T(8,128)(2,1)} %param.4), channel_id=2, replica_groups=mesh['g'=32,'s'=4,'z'=2,'c'=2] {'z','c'}, dimensions={0}, use_global_device_ids=true | all-gather | bytes 491520 | tf_op jit(solution)/shard_map/all_gather | solution.py:194
  10.1 0.0 collective-permute-done
  10.1 1.3 %collective-permute-start.2 = (bf16[4,2,192,128]{3,2,1,0:T(8,128)(2,1)S(1)}, bf16[4,2,192,128]{3,2,1,0:T(8,128)(2,1)S(1)}, u32[]{:S(2)}, u32[]{:S(2)}) collective-permute-start(bf16[4,2,192,128]{3,2,1,0:T(8,128)(2,1)S(1)} %bitcast.7), channel_id=1, source_target_pairs={{0,4},{2,6},{4,8},{6,10},{8,12},{1,13},{10,14},{3,15},{16,20},{18,... | collective-permute-start | bytes 1179656 | tf_op jit(solution)/shard_map/ppermute | solution.py:175
  11.4 1.9 %all-gather.1 = bf16[4,192,128]{2,1,0:T(8,128)(2,1)S(1)} all-gather(bf16[2,192,128]{2,1,0:T(8,128)(2,1)S(1)} %collective-permute-done), channel_id=3, replica_groups=mesh['g'=32,'s'=4,'z'=2,'c'=2] {'c'}, dimensions={0}, use_global_device_ids=true | all-gather | bytes 294912 | tf_op jit(solution)/shard_map/all_gather | solution.py:197
  13.4 3.2 %collective-permute-start.1 = (bf16[2,2,192,128]{3,2,1,0:T(8,128)(2,1)S(1)}, bf16[2,2,192,128]{3,2,1,0:T(8,128)(2,1)S(1)}, u32[]{:S(2)}, u32[]{:S(2)}) collective-permute-start(bf16[2,2,192,128]{3,2,1,0:T(8,128)(2,1)S(1)} %bitcast.9), channel_id=1, source_target_pairs={{10,8},{11,9},{8,10},{9,11},{14,12},{15,13},{12,14},{13,15},{26,24... | collective-permute-start | bytes 589832 | tf_op jit(solution)/shard_map/ppermute | solution.py:175
  16.5 0.0 copy-start.1
  16.6 0.7 %copy-done.1 = s32[768]{0:T(1024)S(1)} copy-done((s32[768]{0:T(1024)S(1)}, s32[768]{0:T(1024)}, u32[]{:S(2)}) %copy-start.1) | copy-done | bytes 3096
  17.2 0.7 %shard_map.50 = (f32[1536,128]{1,0:T(8,128)S(1)}, s32[4]{0:T(128)S(1)}) custom-call(s32[6,128]{1,0:T(8,128)S(1)} %bitcast.13), custom_call_target="tpu_custom_call" | custom-call | flops 400000000 | bytes 1000000 | tf_op jit(solution)/shard_map/pallas_call | solution.py:200
  18.0 0.0 copy-done
  18.0 1.3 %shard_map.51 = (f32[1536,128]{1,0:T(8,128)S(1)}, f32[1536,256]{1,0:T(8,128)S(1)}) custom-call(f32[1536,128]{1,0:T(8,128)S(1)} %get-tuple-element.17.cols_ref, bf16[1536,128]{1,0:T(8,128)(2,1)S(1)} %bitcast.11, bf16[4,2,192,128]{3,2,1,0:T(8,128)(2,1)S(1)} %bitcast.8), custom_call_target="tpu_custom_call" | custom-call | flops 600000000 | bytes 4000000 | tf_op jit(solution)/shard_map/pallas_call | solution.py:208
  19.3 1.7 %collective-permute-done.2 = bf16[4,2,192,128]{3,2,1,0:T(8,128)(2,1)S(1)} collective-permute-done((bf16[4,2,192,128]{3,2,1,0:T(8,128)(2,1)S(1)}, bf16[4,2,192,128]{3,2,1,0:T(8,128)(2,1)S(1)}, u32[]{:S(2)}, u32[]{:S(2)}) %collective-permute-start.2) | collective-permute-done | bytes 393248 | tf_op jit(solution)/shard_map/ppermute | solution.py:175
  21.0 2.4 %all-gather.2 = bf16[8,2,192,128]{3,2,1,0:T(8,128)(2,1)S(1)} all-gather(bf16[4,2,192,128]{3,2,1,0:T(8,128)(2,1)S(1)} %collective-permute-done.2), channel_id=4, replica_groups=mesh['g'=32,'s'=4,'z'=2,'c'=2] {'c'}, dimensions={0}, use_global_device_ids=true | all-gather | bytes 1179648 | tf_op jit(solution)/shard_map/all_gather | solution.py:216
  23.3 0.0 collective-permute-done.1.over_ref
  23.3 5.9 %shard_map.52 = (bf16[1536,128]{1,0:T(8,128)(2,1)}, f32[2,768]{1,0:T(2,128)}) custom-call(s32[4]{0:T(128)S(1)} %get-tuple-element.14.first_ref, bf16[1536,128]{1,0:T(8,128)(2,1)S(1)} %bitcast.12, bf16[2,2,192,128]{3,2,1,0:T(8,128)(2,1)S(1)} %bitcast.10, bf16[2,2,192,128]{3,2,1,0:T(8,128)(2,1)S(1)} %collective-permute-done.1.over_ref, ...), custom_call_target="tpu_custom_call" | custom-call | flops 4000000000 | bytes 6000000 | tf_op jit(solution)/shard_map/pallas_call | solution.py:217
Async XLA Ops:
  0.6 17.4 %copy-start = (bf16[768,2,128]{2,1,0:T(2,128)(2,1)S(1)}, bf16[768,2,128]{2,1,0:T(2,128)(2,1)}, u32[]{:S(2)}) copy-start(bf16[768,2,128]{2,1,0:T(2,128)(2,1)} %param.3) | copy-start | bytes 1179652
  0.6 9.5 %collective-permute-start = (bf16[2,192,128]{2,1,0:T(8,128)(2,1)}, bf16[2,192,128]{2,1,0:T(8,128)(2,1)S(1)}, u32[]{:S(2)}, u32[]{:S(2)}) collective-permute-start(bf16[2,192,128]{2,1,0:T(8,128)(2,1)} %param.4), channel_id=1, source_target_pairs={{0,8},{1,9},{2,10},{3,11},{4,12},{5,13},{6,14},{7,15},{16,24},{17,... | collective-permute-start | bytes 294920 | tf_op jit(solution)/shard_map/ppermute | solution.py:175
  10.1 10.8 %collective-permute-start.2 = (bf16[4,2,192,128]{3,2,1,0:T(8,128)(2,1)S(1)}, bf16[4,2,192,128]{3,2,1,0:T(8,128)(2,1)S(1)}, u32[]{:S(2)}, u32[]{:S(2)}) collective-permute-start(bf16[4,2,192,128]{3,2,1,0:T(8,128)(2,1)S(1)} %bitcast.7), channel_id=1, source_target_pairs={{0,4},{2,6},{4,8},{6,10},{8,12},{1,13},{10,14},{3,15},{16,20},{18,... | collective-permute-start | bytes 1179656 | tf_op jit(solution)/shard_map/ppermute | solution.py:175
  13.4 9.9 %collective-permute-start.1 = (bf16[2,2,192,128]{3,2,1,0:T(8,128)(2,1)S(1)}, bf16[2,2,192,128]{3,2,1,0:T(8,128)(2,1)S(1)}, u32[]{:S(2)}, u32[]{:S(2)}) collective-permute-start(bf16[2,2,192,128]{3,2,1,0:T(8,128)(2,1)S(1)} %bitcast.9), channel_id=1, source_target_pairs={{10,8},{11,9},{8,10},{9,11},{14,12},{15,13},{12,14},{13,15},{26,24... | collective-permute-start | bytes 589832 | tf_op jit(solution)/shard_map/ppermute | solution.py:175
  16.5 0.7 %copy-start.1 = (s32[768]{0:T(1024)S(1)}, s32[768]{0:T(1024)}, u32[]{:S(2)}) copy-start(s32[768]{0:T(1024)} %param.5) | copy-start | bytes 9220

commit v8 on v7

--- a/solution.py
+++ b/solution.py
@@ -86,7 +86,7 @@
 
 
 def row_blocks(count):
-    parts, blocks, first = (2, 3, 3, 3, 1), [], 0
+    parts, blocks, first = (1, 3, 3, 3, 2), [], 0
     for part in parts:
         blocks.append((first, count * part // sum(parts)))
         first += blocks[-1][1]

time: 29.4 us -> 29.6 us (level)
  no operation moved by 1% of the time
where the time goes in v8:
time: 29.6 us; the launch traced here: 29.4 us
  blocking collectives  12.4 us (42%)
  Pallas kernels  8.1 us (27%)
  starting transfers between devices  5.87 us (20%)
  waiting for transfers between devices  1.68 us (6%)
  local copies, waits for them, and re-layouts  0.69 us (2%)
  between operations  0.69 us (2%)
    all_gather x1, blocking collectives, per_device(): own = lax.all_gather(keys_values, ('z', 'c'), axis=0)  8.06 us
    pallas_call x1, Pallas kernels, per_device(): pl.pallas_call(functools.partial(earlier_kernel, heads, row_blocks(count)...  6.07 us
    ppermute x3, starting transfers between devices, permuted(): return lax.ppermute(value, ('s', 'z', 'c'), pairs)  5.87 us
    all_gather x1, blocking collectives, per_device(): near = lax.all_gather(near, 'c', axis=0)  2.36 us
    all_gather x1, blocking collectives, per_device(): far = lax.all_gather(far, 'c', axis=0)  1.95 us
    ppermute x3, waiting for transfers between devices, permuted(): return lax.ppermute(value, ('s', 'z', 'c'), pairs)  1.68 us
    pallas_call x1, Pallas kernels, per_device(): pl.pallas_call(functools.partial(own_kernel, heads, scale), out_shape=sta...  1.28 us
    pallas_call x1, Pallas kernels, per_device(): pl.pallas_call(functools.partial(starts_kernel, heads), out_shape=(state[...  0.75 us
  transfers between devices with their start and end apart: 3, of which 1 were waited for; matrix products, arithmetic and copies ran while one was open for 0% of the time, Pallas kernels for 7%

profile of v8, /device:TPU:7, one launch (start us, length us, event | category | flops | bytes accessed | tf_op | source)
XLA Modules:
  0.0 29.4 jit_solution(7889406014673644623)
XLA Ops:
  0.6 0.0 copy-start
  0.6 1.4 %collective-permute-start = (bf16[2,192,128]{2,1,0:T(8,128)(2,1)}, bf16[2,192,128]{2,1,0:T(8,128)(2,1)S(1)}, u32[]{:S(2)}, u32[]{:S(2)}) collective-permute-start(bf16[2,192,128]{2,1,0:T(8,128)(2,1)} %param.4), channel_id=1, source_target_pairs={{0,8},{1,9},{2,10},{3,11},{4,12},{5,13},{6,14},{7,15},{16,24},{17,... | collective-permute-start | bytes 294920 | tf_op jit(solution)/shard_map/ppermute | solution.py:175
  2.1 8.1 %all-gather = bf16[8,192,128]{2,1,0:T(8,128)(2,1)S(1)} all-gather(bf16[2,192,128]{2,1,0:T(8,128)(2,1)} %param.4), channel_id=2, replica_groups=mesh['g'=32,'s'=4,'z'=2,'c'=2] {'z','c'}, dimensions={0}, use_global_device_ids=true | all-gather | bytes 491520 | tf_op jit(solution)/shard_map/all_gather | solution.py:194
  10.1 0.0 collective-permute-done
  10.1 1.3 %collective-permute-start.2 = (bf16[4,2,192,128]{3,2,1,0:T(8,128)(2,1)S(1)}, bf16[4,2,192,128]{3,2,1,0:T(8,128)(2,1)S(1)}, u32[]{:S(2)}, u32[]{:S(2)}) collective-permute-start(bf16[4,2,192,128]{3,2,1,0:T(8,128)(2,1)S(1)} %bitcast.7), channel_id=1, source_target_pairs={{0,4},{2,6},{4,8},{6,10},{8,12},{1,13},{10,14},{3,15},{16,20},{18,... | collective-permute-start | bytes 1179656 | tf_op jit(solution)/shard_map/ppermute | solution.py:175
  11.4 1.9 %all-gather.1 = bf16[4,192,128]{2,1,0:T(8,128)(2,1)S(1)} all-gather(bf16[2,192,128]{2,1,0:T(8,128)(2,1)S(1)} %collective-permute-done), channel_id=3, replica_groups=mesh['g'=32,'s'=4,'z'=2,'c'=2] {'c'}, dimensions={0}, use_global_device_ids=true | all-gather | bytes 294912 | tf_op jit(solution)/shard_map/all_gather | solution.py:197
  13.4 3.2 %collective-permute-start.1 = (bf16[2,2,192,128]{3,2,1,0:T(8,128)(2,1)S(1)}, bf16[2,2,192,128]{3,2,1,0:T(8,128)(2,1)S(1)}, u32[]{:S(2)}, u32[]{:S(2)}) collective-permute-start(bf16[2,2,192,128]{3,2,1,0:T(8,128)(2,1)S(1)} %bitcast.9), channel_id=1, source_target_pairs={{10,8},{11,9},{8,10},{9,11},{14,12},{15,13},{12,14},{13,15},{26,24... | collective-permute-start | bytes 589832 | tf_op jit(solution)/shard_map/ppermute | solution.py:175
  16.5 0.0 copy-start.1
  16.6 0.7 %copy-done.1 = s32[768]{0:T(1024)S(1)} copy-done((s32[768]{0:T(1024)S(1)}, s32[768]{0:T(1024)}, u32[]{:S(2)}) %copy-start.1) | copy-done | bytes 3096
  17.2 0.7 %shard_map.50 = (f32[1536,128]{1,0:T(8,128)S(1)}, s32[4]{0:T(128)S(1)}) custom-call(s32[6,128]{1,0:T(8,128)S(1)} %bitcast.13), custom_call_target="tpu_custom_call" | custom-call | flops 400000000 | bytes 1000000 | tf_op jit(solution)/shard_map/pallas_call | solution.py:200
  18.0 0.0 copy-done
  18.0 1.3 %shard_map.51 = (f32[1536,128]{1,0:T(8,128)S(1)}, f32[1536,256]{1,0:T(8,128)S(1)}) custom-call(f32[1536,128]{1,0:T(8,128)S(1)} %get-tuple-element.17.cols_ref, bf16[1536,128]{1,0:T(8,128)(2,1)S(1)} %bitcast.11, bf16[4,2,192,128]{3,2,1,0:T(8,128)(2,1)S(1)} %bitcast.8), custom_call_target="tpu_custom_call" | custom-call | flops 600000000 | bytes 4000000 | tf_op jit(solution)/shard_map/pallas_call | solution.py:208
  19.3 1.7 %collective-permute-done.2 = bf16[4,2,192,128]{3,2,1,0:T(8,128)(2,1)S(1)} collective-permute-done((bf16[4,2,192,128]{3,2,1,0:T(8,128)(2,1)S(1)}, bf16[4,2,192,128]{3,2,1,0:T(8,128)(2,1)S(1)}, u32[]{:S(2)}, u32[]{:S(2)}) %collective-permute-start.2) | collective-permute-done | bytes 393248 | tf_op jit(solution)/shard_map/ppermute | solution.py:175
  21.0 2.4 %all-gather.2 = bf16[8,2,192,128]{3,2,1,0:T(8,128)(2,1)S(1)} all-gather(bf16[4,2,192,128]{3,2,1,0:T(8,128)(2,1)S(1)} %collective-permute-done.2), channel_id=4, replica_groups=mesh['g'=32,'s'=4,'z'=2,'c'=2] {'c'}, dimensions={0}, use_global_device_ids=true | all-gather | bytes 1179648 | tf_op jit(solution)/shard_map/all_gather | solution.py:216
  23.3 0.0 collective-permute-done.1.over_ref
  23.3 6.1 %shard_map.52 = (bf16[1536,128]{1,0:T(8,128)(2,1)}, f32[2,768]{1,0:T(2,128)}) custom-call(s32[4]{0:T(128)S(1)} %get-tuple-element.14.first_ref, bf16[1536,128]{1,0:T(8,128)(2,1)S(1)} %bitcast.12, bf16[2,2,192,128]{3,2,1,0:T(8,128)(2,1)S(1)} %bitcast.10, bf16[2,2,192,128]{3,2,1,0:T(8,128)(2,1)S(1)} %collective-permute-done.1.over_ref, ...), custom_call_target="tpu_custom_call" | custom-call | flops 4000000000 | bytes 6000000 | tf_op jit(solution)/shard_map/pallas_call | solution.py:217
Async XLA Ops:
  0.6 17.4 %copy-start = (bf16[768,2,128]{2,1,0:T(2,128)(2,1)S(1)}, bf16[768,2,128]{2,1,0:T(2,128)(2,1)}, u32[]{:S(2)}) copy-start(bf16[768,2,128]{2,1,0:T(2,128)(2,1)} %param.3) | copy-start | bytes 1179652
  0.6 9.5 %collective-permute-start = (bf16[2,192,128]{2,1,0:T(8,128)(2,1)}, bf16[2,192,128]{2,1,0:T(8,128)(2,1)S(1)}, u32[]{:S(2)}, u32[]{:S(2)}) collective-permute-start(bf16[2,192,128]{2,1,0:T(8,128)(2,1)} %param.4), channel_id=1, source_target_pairs={{0,8},{1,9},{2,10},{3,11},{4,12},{5,13},{6,14},{7,15},{16,24},{17,... | collective-permute-start | bytes 294920 | tf_op jit(solution)/shard_map/ppermute | solution.py:175
  10.1 10.8 %collective-permute-start.2 = (bf16[4,2,192,128]{3,2,1,0:T(8,128)(2,1)S(1)}, bf16[4,2,192,128]{3,2,1,0:T(8,128)(2,1)S(1)}, u32[]{:S(2)}, u32[]{:S(2)}) collective-permute-start(bf16[4,2,192,128]{3,2,1,0:T(8,128)(2,1)S(1)} %bitcast.7), channel_id=1, source_target_pairs={{0,4},{2,6},{4,8},{6,10},{8,12},{1,13},{10,14},{3,15},{16,20},{18,... | collective-permute-start | bytes 1179656 | tf_op jit(solution)/shard_map/ppermute | solution.py:175
  13.4 9.9 %collective-permute-start.1 = (bf16[2,2,192,128]{3,2,1,0:T(8,128)(2,1)S(1)}, bf16[2,2,192,128]{3,2,1,0:T(8,128)(2,1)S(1)}, u32[]{:S(2)}, u32[]{:S(2)}) collective-permute-start(bf16[2,2,192,128]{3,2,1,0:T(8,128)(2,1)S(1)} %bitcast.9), channel_id=1, source_target_pairs={{10,8},{11,9},{8,10},{9,11},{14,12},{15,13},{12,14},{13,15},{26,24... | collective-permute-start | bytes 589832 | tf_op jit(solution)/shard_map/ppermute | solution.py:175
  16.5 0.7 %copy-start.1 = (s32[768]{0:T(1024)S(1)}, s32[768]{0:T(1024)}, u32[]{:S(2)}) copy-start(s32[768]{0:T(1024)} %param.5) | copy-start | bytes 9220
